TPU v7x, 32 devices: a whole 2x2x4 slice. The times are simulated.
32 devices in a mesh: utt: 4 (over y, core), seq: 8 (over z, x).
Axes of the slice: x: 2, y: 2, z: 4, core: 2. Of those that a mesh axis runs over, the one named last changes fastest.
Arguments:
- frames: float32 [8, 1024, 512], P('utt', 'seq'), may hold values from -6 to 6
- lengths: int32 [8], P('utt'), may hold values from 256 to 1024, as said below
- out_grad: float32 [8, 1024, 512], P('utt', 'seq'), may hold values from -6 to 6
- norm_gain: bfloat16 [5, 512], replicated, may hold values from 0.5 to 1.5
- norm_bias: bfloat16 [5, 512], replicated, may hold values from -1 to 1
- feed_in: bfloat16 [2, 512, 2048], replicated, may hold values from -0.25 to 0.25
- feed_in_bias: bfloat16 [2, 2048], replicated, may hold values from -1 to 1
- feed_out: bfloat16 [2, 2048, 512], replicated, may hold values from -0.125 to 0.125
- feed_out_bias: bfloat16 [2, 512], replicated, may hold values from -1 to 1
- attend_in: bfloat16 [4, 512, 512], replicated, may hold values from -0.25 to 0.25
- attend_vectors: bfloat16 [5, 512], replicated, may hold values from -1.5 to 1.5
- attend_out: bfloat16 [512, 512], replicated, may hold values from -1 to 1
- mixer_in: bfloat16 [512, 1024], replicated, may hold values from -0.25 to 0.25
- mixer_in_bias: bfloat16 [1024], replicated, may hold values from -1 to 1
- depthwise: bfloat16 [512, 9], replicated, may hold values from -2 to 2
- mixer_vectors: bfloat16 [2, 512], replicated, may hold values from -1 to 1
- mixer_out: bfloat16 [512, 512], replicated, may hold values from -0.25 to 0.25
- batch_gain: bfloat16 [512], replicated, may hold values from 0.5 to 1.5
- batch_shift: bfloat16 [512], replicated, may hold values from -1 to 1
- running_mean: float32 [512], replicated, may hold values from -0.08 to 0.08
- running_variance: float32 [512], replicated, may hold values from 0.004 to 0.04
Outputs:
- layer_output: float32 [8, 1024, 512], P('utt', 'seq')
- frames_grad: float32 [8, 1024, 512], P('utt', 'seq')
- norm_gain_grad: float32 [5, 512], replicated
- norm_bias_grad: float32 [5, 512], replicated
- feed_in_grad: float32 [2, 512, 2048], replicated
- feed_in_bias_grad: float32 [2, 2048], replicated
- feed_out_grad: float32 [2, 2048, 512], replicated
- feed_out_bias_grad: float32 [2, 512], replicated
- attend_in_grad: float32 [4, 512, 512], replicated
- attend_vectors_grad: float32 [5, 512], replicated
- attend_out_grad: float32 [512, 512], replicated
- mixer_in_grad: float32 [512, 1024], replicated
- mixer_in_bias_grad: float32 [1024], replicated
- depthwise_grad: float32 [512, 9], replicated
- mixer_vectors_grad: float32 [2, 512], replicated
- mixer_out_grad: float32 [512, 512], replicated
- batch_gain_grad: float32 [512], replicated
- batch_shift_grad: float32 [512], replicated
- new_mean: float32 [512], replicated
- new_variance: float32 [512], replicated
Inputs may be any that keep to these rules, and one draw needn't show every extreme that they name: `lengths`: in each aligned block of 2 utterances (those of one index of utt) at least one has exactly 1024 frames.
All inputs are finite; a program needn't handle non-finite values.
Results may differ from a plain program's by a relative error of at most 0.025.
Values may be sent and summed in bfloat16 or wider, within the bound.
No kernel may reach another device: no remote copies, remote signals or barrier semaphores. Data moves between devices by JAX's collectives and lax.ppermute only.
A program may use at most 320 MiB of HBM per device.

v0:
```python
import math

import jax
import jax.numpy as jnp
from jax import lax
from jax.sharding import PartitionSpec as P

HEADS = 8
KERNEL = 9
HEAD_DIM = 64


TOP_PRECISION = lax.Precision.HIGHEST
EPSILON = 1e-05


def with_halo(cells, sides, width):
    for axis, dim in sides:
        count = lax.axis_size(axis)
        ends = count - 1
        head = lax.slice_in_dim(cells, 0, width, axis=dim)
        tail = lax.slice_in_dim(cells, cells.shape[dim] - width, cells.shape[dim], axis=dim)
        cells = jnp.concatenate(
            [
                lax.ppermute(tail, axis, [(i, (i + 1) % count) for i in range(ends)]),
                cells,
                lax.ppermute(head, axis, [((i + 1) % count, i) for i in range(ends)]),
            ],
            axis=dim,
        )
    return cells


def project(first_operand, second_operand):
    return jnp.dot(first_operand, second_operand, preferred_element_type=jnp.float32)


def outer_sum(first_operand, second_operand):
    return jnp.einsum(
        "ufd,ufe->de", first_operand, second_operand, preferred_element_type=jnp.float32
    )


def project_back(grad_rows, weight):
    return jnp.einsum("ufe,de->ufd", grad_rows, weight, preferred_element_type=jnp.float32)


def column_sum(grad_rows):
    return jnp.sum(grad_rows.astype(jnp.float32), axis=(0, 1))


def flatten_grads(members):
    flattened = jnp.concatenate([member.reshape(-1) for member in members])
    return flattened


def restore_grads(flattened, members):
    restored = []
    offset = 0
    for member in members:
        element_count = member.size
        restored.append(flattened[offset : offset + element_count].reshape(member.shape))
        offset = offset + element_count
    return tuple(restored)


def norm_forward(values, gain_vector, shift_vector):
    average = jnp.mean(values, axis=-1, keepdims=True)
    centered = values - average
    spread = jnp.mean(centered * centered, axis=-1, keepdims=True)
    inverse = lax.rsqrt(spread + EPSILON)
    normed = centered * inverse
    return (
        normed * gain_vector.astype(jnp.float32) + shift_vector.astype(jnp.float32),
        normed,
        inverse,
    )


def norm_backward(grad_rows, normed, inverse, gain_vector):
    scaled = grad_rows * gain_vector.astype(jnp.float32)
    row_inner = (
        scaled
        - jnp.mean(scaled, axis=-1, keepdims=True)
        - normed * jnp.mean(scaled * normed, axis=-1, keepdims=True)
    )
    return (
        row_inner * inverse,
        jnp.sum(grad_rows * normed, axis=(0, 1)),
        jnp.sum(grad_rows, axis=(0, 1)),
    )


def silu_slope(preact):
    logistic = jax.nn.sigmoid(preact)
    return logistic * (1.0 + preact * (1.0 - logistic))


def feed_forward(values, gain_vector, shift_vector, weight_in, bias_in, weight_out, bias_out):
    normed_out, normed, inverse = norm_forward(values, gain_vector, shift_vector)
    hidden = normed_out.astype(jnp.bfloat16)
    preact = project(hidden, weight_in) + bias_in.astype(jnp.float32)
    active = jax.nn.silu(preact).astype(jnp.bfloat16)
    return (
        project(active, weight_out) + bias_out.astype(jnp.float32),
        (normed, inverse, hidden, preact, active),
    )


def feed_backward(grad_rows, stored, gain_vector, weight_in, weight_out):
    normed, inverse, hidden, preact, active = stored
    grad_low = grad_rows.astype(jnp.bfloat16)
    grad_weight_out = outer_sum(active, grad_low)
    grad_bias_out = column_sum(grad_low)
    grad_pre = (project_back(grad_low, weight_out) * silu_slope(preact)).astype(jnp.bfloat16)
    grad_weight_in = outer_sum(hidden, grad_pre)
    grad_bias_in = column_sum(grad_pre)
    grad_values, grad_gain, grad_shift = norm_backward(
        project_back(grad_pre, weight_in), normed, inverse, gain_vector
    )
    return (
        grad_values,
        grad_gain,
        grad_shift,
        grad_weight_in,
        grad_bias_in,
        grad_weight_out,
        grad_bias_out,
    )


def position_table(row_total, top_offset, feature_count):
    offsets = (top_offset - jnp.arange(row_total, dtype=jnp.int32)).astype(jnp.float32)
    halves = jnp.arange(feature_count // 2, dtype=jnp.int32).astype(jnp.float32)
    frequencies = jnp.exp(halves * (-2.0 * math.log(10000.0) / feature_count))
    angles = offsets[:, None] * frequencies[None, :]
    return jnp.stack([jnp.sin(angles), jnp.cos(angles)], axis=-1).reshape(row_total, feature_count)


def skew(before_skewing, length):
    leading = before_skewing.shape[:-2]
    row_count, col_count = (before_skewing.shape[-2], before_skewing.shape[-1])
    flattened = before_skewing.reshape(leading + (row_count * col_count,))
    flattened = jnp.pad(flattened, [(0, 0)] * len(leading) + [(0, row_count)])
    return flattened.reshape(leading + (row_count, col_count + 1))[..., :length]


def unskew(placed, col_count):
    leading = placed.shape[:-2]
    row_count, length = (placed.shape[-2], placed.shape[-1])
    widened = jnp.pad(placed, [(0, 0)] * len(leading) + [(0, 0), (0, col_count + 1 - length)])
    flattened = widened.reshape(leading + (row_count * (col_count + 1),))[
        ..., : row_count * col_count
    ]
    return flattened.reshape(leading + (row_count, col_count))


def block_scores(content, relative_offset, key_rows, limits, relative_offsets):
    key_count = key_rows.shape[1]
    direct = jnp.einsum("uqhd,ukhd->uhqk", content, key_rows, preferred_element_type=jnp.float32)
    before_skewing = jnp.einsum(
        "zywj,bwj->zwyb",
        relative_offset[:, ::-1],
        relative_offsets,
        preferred_element_type=jnp.float32,
    )
    placed = skew(before_skewing, key_count)[:, :, ::-1]
    scores = (direct + placed) * HEAD_DIM ** (-0.5)
    allowed = (
        jnp.arange(key_count, dtype=jnp.int32)[None, None, None, :] < limits[:, None, None, None]
    )
    return jnp.where(allowed, scores, -1000000000.0)


def attend_block(pieces, relative_offsets):
    content, relative_offset, key_rows, value_rows, limits = pieces
    scores = block_scores(content, relative_offset, key_rows, limits, relative_offsets)
    highest = jnp.max(scores, axis=-1, keepdims=True)
    shifted = jnp.exp(scores - highest)
    totals = jnp.sum(shifted, axis=-1, keepdims=True)
    weights = (shifted / totals).astype(jnp.bfloat16)
    attended = jnp.einsum(
        "uhqk,ukhd->uqhd", weights, value_rows, preferred_element_type=jnp.float32
    )
    return (attended, highest + jnp.log(totals))


def attend_block_back(accumulated, pieces, relative_offsets):
    content, relative_offset, key_rows, value_rows, limits, log_totals, grad_attended = pieces
    scores = block_scores(content, relative_offset, key_rows, limits, relative_offsets)
    weights = jnp.exp(scores - log_totals)
    grad_weights = jnp.einsum(
        "uqhd,ukhd->uhqk", grad_attended, value_rows, preferred_element_type=jnp.float32
    )
    row_inner = jnp.sum(weights * grad_weights, axis=-1, keepdims=True)
    grad_scores = (weights * (grad_weights - row_inner) * HEAD_DIM ** (-0.5)).astype(jnp.bfloat16)
    grad_content = jnp.einsum(
        "uhqk,ukhd->uqhd", grad_scores, key_rows, preferred_element_type=jnp.float32
    )
    gradient_before_skewing = unskew(grad_scores[:, :, ::-1], relative_offsets.shape[0])
    grad_position = jnp.einsum(
        "nrwy,yrv->nwrv",
        gradient_before_skewing,
        relative_offsets,
        preferred_element_type=jnp.float32,
    )[:, ::-1]
    accumulated = accumulated + jnp.einsum(
        "plrb,prlx->blx",
        gradient_before_skewing,
        relative_offset[:, ::-1],
        preferred_element_type=jnp.float32,
    )
    outputs = (grad_content, grad_position, row_inner)
    grad_values = jnp.einsum(
        "uhqk,uqhd->ukhd",
        weights.astype(jnp.bfloat16),
        grad_attended,
        preferred_element_type=jnp.float32,
    )
    grad_keys = jnp.einsum(
        "uhqk,uqhd->ukhd", grad_scores, content, preferred_element_type=jnp.float32
    )
    outputs = outputs + (grad_keys, grad_values)
    return (accumulated, outputs)


def shards(
    frames,
    lengths,
    out_grad,
    norm_gain,
    norm_bias,
    feed_in,
    feed_in_bias,
    feed_out,
    feed_out_bias,
    attend_in,
    attend_vectors,
    attend_out,
    mixer_in,
    mixer_in_bias,
    depthwise,
    mixer_vectors,
    mixer_out,
    batch_gain,
    batch_shift,
    running_mean,
    running_variance,
):
    utt_rows, block_frames, features = frames.shape
    seq_count = lax.axis_size("seq")
    frames_all = block_frames * seq_count
    first_frame = lax.axis_index("seq") * block_frames
    window = block_frames + frames_all - 1
    per_block = min(utt_rows, max(1, 512 // block_frames))
    blocks = utt_rows // per_block
    frame_mask = (
        (first_frame + jnp.arange(block_frames, dtype=jnp.int32))[None, :] < lengths[:, None]
    ).astype(jnp.float32)
    mask_cols = frame_mask[..., None]

    def blocked(source):
        return source.reshape((blocks, per_block) + source.shape[1:-1] + (HEADS, HEAD_DIM))

    limit_blocks = lengths.reshape(blocks, per_block)
    first_out, first_stored = feed_forward(
        frames,
        norm_gain[0],
        norm_bias[0],
        feed_in[0],
        feed_in_bias[0],
        feed_out[0],
        feed_out_bias[0],
    )
    after_first = frames + 0.5 * first_out
    attend_normed, normed_two, inverse_two = norm_forward(after_first, norm_gain[1], norm_bias[1])
    hidden_two = attend_normed.astype(jnp.bfloat16)
    queries = project(hidden_two, attend_in[0]) + attend_vectors[0].astype(jnp.float32)
    key_rows = project(hidden_two, attend_in[1]).astype(jnp.bfloat16)
    value_rows = (project(hidden_two, attend_in[2]) + attend_vectors[1].astype(jnp.float32)).astype(
        jnp.bfloat16
    )
    content = (queries + attend_vectors[3].astype(jnp.float32)).astype(jnp.bfloat16)
    relative_offset = (queries + attend_vectors[4].astype(jnp.float32)).astype(jnp.bfloat16)
    key_all, value_all = (
        lax.all_gather(key_rows, "seq", axis=1, tiled=True),
        lax.all_gather(value_rows, "seq", axis=1, tiled=True),
    )
    table_low = position_table(window, first_frame + block_frames - 1, features).astype(
        jnp.bfloat16
    )
    relative_offsets = (
        project(table_low, attend_in[3]).astype(jnp.bfloat16).reshape(window, HEADS, HEAD_DIM)
    )
    attended, log_totals = lax.map(
        lambda pieces: attend_block(pieces, relative_offsets),
        (
            blocked(content),
            blocked(relative_offset),
            blocked(key_all),
            blocked(value_all),
            limit_blocks,
        ),
    )
    attended_low = attended.reshape(utt_rows, block_frames, features).astype(jnp.bfloat16)
    after_attend = (
        after_first + project(attended_low, attend_out) + attend_vectors[2].astype(jnp.float32)
    )
    mixer_normed, normed_three, inverse_three = norm_forward(
        after_attend, norm_gain[2], norm_bias[2]
    )
    hidden_three = mixer_normed.astype(jnp.bfloat16)
    mixer_pre = project(hidden_three, mixer_in) + mixer_in_bias.astype(jnp.float32)
    linear_half = mixer_pre[..., :features]
    gate_half = jax.nn.sigmoid(mixer_pre[..., features:])
    gated_units = (linear_half * gate_half * mask_cols).astype(jnp.bfloat16)
    margin = KERNEL // 2
    widened = with_halo(gated_units, (("seq", 1),), margin)
    kernel_rows = depthwise.astype(jnp.float32)
    convolved = mixer_vectors[0].astype(jnp.float32) + sum(
        (
            kernel_rows[:, offset] * widened[:, offset : offset + block_frames].astype(jnp.float32)
            for offset in range(KERNEL)
        )
    )
    mask_total = jnp.sum(frame_mask)
    total_sum, valid_count = lax.psum(
        (jnp.sum(convolved * mask_cols, axis=(0, 1)), mask_total), ("utt", "seq")
    )
    average = total_sum / valid_count
    centered = convolved - average
    variance = (
        lax.psum(jnp.sum(centered * centered * mask_cols, axis=(0, 1)), ("utt", "seq"))
        / valid_count
    )
    inverse_batch = lax.rsqrt(variance + EPSILON)
    normed_batch = centered * inverse_batch
    batch_out = normed_batch * batch_gain.astype(jnp.float32) + batch_shift.astype(jnp.float32)
    swished = jax.nn.silu(batch_out).astype(jnp.bfloat16)
    after_mixer = after_attend + project(swished, mixer_out) + mixer_vectors[1].astype(jnp.float32)
    second_out, second_stored = feed_forward(
        after_mixer,
        norm_gain[3],
        norm_bias[3],
        feed_in[1],
        feed_in_bias[1],
        feed_out[1],
        feed_out_bias[1],
    )
    after_second = after_mixer + 0.5 * second_out
    layer_output, normed_last, inverse_last = norm_forward(after_second, norm_gain[4], norm_bias[4])
    grad_second, gain_last, shift_last = norm_backward(
        out_grad, normed_last, inverse_last, norm_gain[4]
    )
    second_back = feed_backward(
        0.5 * grad_second, second_stored, norm_gain[3], feed_in[1], feed_out[1]
    )
    grad_mixer = grad_second + second_back[0]
    grad_branch = grad_mixer.astype(jnp.bfloat16)
    mixer_out_grad = outer_sum(swished, grad_branch)
    out_bias_grad = column_sum(grad_branch)
    grad_batch = project_back(grad_branch, mixer_out) * silu_slope(batch_out)
    batch_shift_grad, batch_gain_grad = lax.psum(
        (jnp.sum(grad_batch, axis=(0, 1)), jnp.sum(grad_batch * normed_batch, axis=(0, 1))),
        ("utt", "seq"),
    )
    grad_conv = (
        batch_gain.astype(jnp.float32)
        * inverse_batch
        * (
            grad_batch
            - mask_cols / valid_count * (batch_shift_grad + normed_batch * batch_gain_grad)
        )
    ).astype(jnp.bfloat16)
    grad_wide = with_halo(grad_conv, (("seq", 1),), margin)
    grad_gated = mask_cols * sum(
        (
            kernel_rows[:, offset]
            * grad_wide[:, 2 * margin - offset : 2 * margin - offset + block_frames].astype(
                jnp.float32
            )
            for offset in range(KERNEL)
        )
    )
    grad_conv_wide = grad_conv.astype(jnp.float32)
    depthwise_grad = jnp.stack(
        [
            jnp.sum(
                grad_conv_wide * widened[:, offset : offset + block_frames].astype(jnp.float32),
                axis=(0, 1),
            )
            for offset in range(KERNEL)
        ],
        axis=1,
    )
    kernel_bias_grad = column_sum(grad_conv)
    grad_mixer_pre = jnp.concatenate(
        [grad_gated * gate_half, grad_gated * linear_half * gate_half * (1.0 - gate_half)], axis=-1
    ).astype(jnp.bfloat16)
    mixer_in_grad = outer_sum(hidden_three, grad_mixer_pre)
    mixer_in_bias_grad = column_sum(grad_mixer_pre)
    grad_three, gain_three, shift_three = norm_backward(
        project_back(grad_mixer_pre, mixer_in), normed_three, inverse_three, norm_gain[2]
    )
    grad_attend = grad_mixer + grad_three
    mixer_vectors_grad = jnp.stack([kernel_bias_grad, out_bias_grad])
    mixer_grads = (
        mixer_in_grad,
        mixer_in_bias_grad,
        depthwise_grad,
        mixer_vectors_grad,
        mixer_out_grad,
    )
    grad_branch_two = grad_attend.astype(jnp.bfloat16)
    attend_out_grad = outer_sum(attended_low, grad_branch_two)
    out_bias_two = column_sum(grad_branch_two)
    grad_attended = project_back(grad_branch_two, attend_out).astype(jnp.bfloat16)
    table_start = jnp.zeros((window, HEADS, HEAD_DIM), jnp.float32)
    table_grad, block_grads = lax.scan(
        lambda accumulated, pieces: attend_block_back(accumulated, pieces, relative_offsets),
        table_start,
        (
            blocked(content),
            blocked(relative_offset),
            blocked(key_all),
            blocked(value_all),
            limit_blocks,
            log_totals,
            blocked(grad_attended),
        ),
    )
    grad_content = block_grads[0].reshape(utt_rows, block_frames, features)
    grad_position = block_grads[1].reshape(utt_rows, block_frames, features)
    grad_keys = block_grads[3].reshape(utt_rows, frames_all, features)
    grad_values = block_grads[4].reshape(utt_rows, frames_all, features)
    key_summed, value_summed = (
        lax.psum_scatter(
            grad_keys.astype(jnp.bfloat16), "seq", scatter_dimension=1, tiled=True
        ).astype(jnp.float32),
        lax.psum_scatter(
            grad_values.astype(jnp.bfloat16), "seq", scatter_dimension=1, tiled=True
        ).astype(jnp.float32),
    )
    key_low = key_summed.astype(jnp.bfloat16)
    value_low = value_summed.astype(jnp.bfloat16)
    query_low = (grad_content + grad_position).astype(jnp.bfloat16)
    position_weight_grad = jnp.einsum(
        "md,me->de",
        table_low.astype(jnp.float32),
        table_grad.reshape(window, features),
        precision=TOP_PRECISION,
    )
    attend_in_grad = jnp.stack(
        [
            outer_sum(hidden_two, query_low),
            outer_sum(hidden_two, key_low),
            outer_sum(hidden_two, value_low),
            position_weight_grad,
        ]
    )
    attend_vectors_grad = jnp.stack(
        [
            column_sum(query_low),
            column_sum(value_low),
            out_bias_two,
            jnp.sum(grad_content, axis=(0, 1)),
            jnp.sum(grad_position, axis=(0, 1)),
        ]
    )
    grad_hidden = (
        project_back(query_low, attend_in[0])
        + project_back(key_low, attend_in[1])
        + project_back(value_low, attend_in[2])
    )
    grad_two, gain_two, shift_two = norm_backward(
        grad_hidden, normed_two, inverse_two, norm_gain[1]
    )
    grad_first = grad_attend + grad_two
    first_back = feed_backward(
        0.5 * grad_first, first_stored, norm_gain[0], feed_in[0], feed_out[0]
    )
    frames_grad = grad_first + first_back[0]
    norm_gain_grad = jnp.stack([first_back[1], gain_two, gain_three, second_back[1], gain_last])
    norm_bias_grad = jnp.stack([first_back[2], shift_two, shift_three, second_back[2], shift_last])
    feed_in_grad = jnp.stack([first_back[3], second_back[3]])
    feed_in_bias_grad = jnp.stack([first_back[4], second_back[4]])
    feed_out_grad = jnp.stack([first_back[5], second_back[5]])
    feed_out_bias_grad = jnp.stack([first_back[6], second_back[6]])
    other_grads = (
        norm_gain_grad,
        norm_bias_grad,
        feed_in_grad,
        feed_in_bias_grad,
        feed_out_grad,
        feed_out_bias_grad,
        attend_in_grad,
        attend_vectors_grad,
        attend_out_grad,
    )
    every_grad = other_grads + mixer_grads
    all_shares = lax.psum_scatter(
        flatten_grads(every_grad), ("utt", "seq"), scatter_dimension=0, tiled=True
    )
    all_grads = restore_grads(
        lax.all_gather(all_shares.astype(jnp.bfloat16), ("utt", "seq"), axis=0, tiled=True).astype(
            all_shares.dtype
        ),
        every_grad,
    )
    other_grads = all_grads[:9]
    mixer_grads = all_grads[9:]
    new_mean = 0.9 * running_mean + 0.1 * average
    new_variance = 0.9 * running_variance + 0.1 * variance * valid_count / (valid_count - 1.0)
    return (
        layer_output,
        frames_grad,
        other_grads[0],
        other_grads[1],
        other_grads[2],
        other_grads[3],
        other_grads[4],
        other_grads[5],
        other_grads[6],
        other_grads[7],
        other_grads[8],
        mixer_grads[0],
        mixer_grads[1],
        mixer_grads[2],
        mixer_grads[3],
        mixer_grads[4],
        batch_gain_grad,
        batch_shift_grad,
        new_mean,
        new_variance,
    )


def solution(mesh):
    return jax.shard_map(
        shards,
        mesh=mesh,
        in_specs=(
            P("utt", "seq", None),
            P("utt"),
            P("utt", "seq", None),
            P(),
            P(),
            P(),
            P(),
            P(),
            P(),
            P(),
            P(),
            P(),
            P(),
            P(),
            P(),
            P(),
            P(),
            P(),
            P(),
            P(),
            P(),
        ),
        out_specs=(
            P("utt", "seq", None),
            P("utt", "seq", None),
            P(),
            P(),
            P(),
            P(),
            P(),
            P(),
            P(),
            P(),
            P(),
            P(),
            P(),
            P(),
            P(),
            P(),
            P(),
            P(),
            P(),
            P(),
        ),
        check_vma=False,
    )
```

profile of v0, /device:TPU:0, one launch (start us, length us, event | category | flops | bytes accessed | tf_op | source)
XLA Modules:
  0.0 1336.6 jit_solution(10662328522988477143)
XLA Ops:
  26.9 34.6 %fusion.58 = (bf16[1151,256,1]{0,2,1:T(2,128)(2,1)S(1)}, bf16[1151,256,1]{0,2,1:T(2,128)(2,1)S(1)}) fusion(f32[1151]{0:T(1024)S(1)} %subtract_convert_fusion, f32[256]{0:T(256)S(1)} %multiply_exponential_fusion), kind=kLoop, calls=%fused_computation.100 | loop fusion | flops 883968 | bytes 1184252 | tf_op jit(solution)/shard_map/convert.23
  68.5 6.0 convolution_bitcast_fusion
  74.6 9.8 copy.98
  84.3 14.0 %reshape.699 = f32[2,8,147328]{2,1,0:T(8,128)} reshape(f32[2,8,128,1151]{3,2,1,0:T(8,128)} %copy.98) | data formatting | bytes 18857984 | tf_op jit(solution)/shard_map/while/body/eval_jaxpr/reshape | solution.py:143
  98.3 4.6 pad.12
  102.9 5.4 copy.142
  108.4 8.5 slice.430
  116.9 63.9 %rev.22 = f32[2,8,128,1024]{3,2,1,0:T(8,128)} reverse(f32[2,8,128,1024]{3,2,1,0:T(8,128)} %slice.430), dimensions={2} | reverse | bytes 16777216 | tf_op jit(solution)/shard_map/while/body/eval_jaxpr/rev | solution.py:167
  181.8 3.0 copy.95
  184.8 5.0 fusion.142
  189.8 3.4 copy-done.2
  195.1 3.9 copy.93
  199.0 5.9 fusion.56
  207.9 4.9 collective-permute-start
  219.8 41.7 %all-reduce.5 = (f32[512]{0:T(512)S(1)}, f32[]{:T(128)}) all-reduce(f32[512]{0:T(512)S(1)} %get-tuple-element.184, f32[]{:T(128)} %fusion.130), channel_id=1, replica_groups=mesh['utt'=4,'seq'=8] {'utt','seq'}, use_global_device_ids=true, to_apply=%region_9.10 | all-reduce | flops 513 | bytes 4104 | tf_op jit(solution)/shard_map/psum | solution.py:327
  264.5 39.8 %psum.37 = f32[512]{0:T(512)S(1)} all-reduce(f32[512]{0:T(512)S(1)} %multiply_reduce_fusion.14), channel_id=1, replica_groups=mesh['utt'=4,'seq'=8] {'utt','seq'}, use_global_device_ids=true, to_apply=%region_13.14 | all-reduce | flops 512 | bytes 4096 | tf_op jit(solution)/shard_map/psum | solution.py:333
  323.4 41.2 %all-reduce.4 = (f32[512]{0:T(512)S(1)}, f32[512]{0:T(512)}) all-reduce(f32[512]{0:T(512)} %get-tuple-element.163, f32[512]{0:T(512)S(1)} %get-tuple-element.162), channel_id=1, replica_groups=mesh['utt'=4,'seq'=8] {'utt','seq'}, use_global_device_ids=true, to_apply=%region_25.26 | all-reduce | flops 1024 | bytes 8192 | tf_op jit(solution)/shard_map/psum | solution.py:363
  368.6 4.8 collective-permute-start.3
  380.1 13.9 %multiply_convert_fusion = bf16[2,8,128,1024]{3,2,1,0:T(8,128)(2,1)} fusion(f32[2,8,128,1024]{3,2,1,0:T(8,128)} %copy-done.2, f32[2,8,128]{2,1,0:T(8,128)S(1)} %log_add_fusion, bf16[2,128,8,64]{1,3,2,0:T(8,128)(2,1)S(1)} %bitcast.313, bf16[2,1024,8,64]{1,3,2,0:T(8,128)(2,1)} %bitcast.312), kind=kOutput, calls=%fused_computation.4 | convolution fusion | flops 551554048 | bytes 14950400 | tf_op jit(solution)/shard_map/while/body/eval_jaxpr/sub | solution.py:196
  393.9 4.2 convolution_convert_fusion.1
  398.1 3.9 copy.102
  402.1 6.3 fusion.25
  408.6 4.0 copy.103
  423.6 60.1 %rev.23 = bf16[2,8,128,1024]{3,2,1,0:T(8,128)(2,1)} reverse(bf16[2,8,128,1024]{3,2,1,0:T(8,128)(2,1)} %multiply_convert_fusion), dimensions={2} | reverse | bytes 8388608 | tf_op jit(solution)/shard_map/while/body/eval_jaxpr/rev | solution.py:200
  483.7 5.0 pad.13
  488.7 5.2 reshape.701
  493.9 4.1 slice.470
  498.0 14.7 %reshape.702 = bf16[2,8,128,1151]{3,2,1,0:T(8,128)(2,1)} reshape(bf16[2,8,147328]{2,1,0:T(8,128)(2,1)} %slice.470) | data formatting | bytes 9428992 | tf_op jit(solution)/shard_map/while/body/eval_jaxpr/reshape | solution.py:155
  512.7 4.3 convolution_bitcast_fusion.12
  518.1 4.7 convert_reduce_fusion.7
  537.7 4.0 reduce-scatter.5.cloned.1.call-done
  544.0 3.0 convolution_bitcast_fusion.2
  555.0 3.3 copy.134
  560.0 4.4 pad_maximum_fusion.1
  564.4 9.1 copy.132
  576.4 5.4 copy.130
  584.6 6.7 constant_dynamic-update-slice_fusion.10
  593.4 4.1 constant_dynamic-update-slice_fusion.8
  604.3 18.1 %dynamic-update-slice.10 = f32[6310912]{0:T(1024)} dynamic-update-slice(f32[6310912]{0:T(1024)} %constant_dynamic-update-slice_fusion.4, f32[524288]{0:T(1024)S(1)} %bitcast.301, s32[]{} %constant.141) | dynamic-update-slice | bytes 4194308
  627.9 407.0 %all-reduce.10 = bf16[6310912]{0:T(1024)(128)(2,1)} all-reduce(f32[6310912]{0:T(1024)} %constant_dynamic-update-slice_fusion), channel_id=4, replica_groups=mesh['utt'=4,'seq'=8] {'utt','seq'}, use_global_device_ids=true, to_apply=%region_66.67.clone | all-reduce | flops 6310912 | bytes 37865472
  1036.2 4.6 broadcast.342
  1040.8 7.3 dynamic-update-slice
  1050.3 229.0 %all-reduce.9.cloned.1.call-done = bf16[6310912]{0:T(1024)(128)(2,1)} async-done(((bf16[6310912]{0:T(1024)(128)(2,1)}), bf16[6310912]{0:T(1024)(128)(2,1)}) %all-reduce.9.cloned.1.call-update) | async-done | bytes 12621840
  1279.3 8.7 fusion.137
  1288.0 9.2 reshape.717
  1297.2 9.3 reshape.719
  1306.6 3.8 slice.477
  1310.4 4.9 reshape.720
  (377 shorter events, 146.2 us)
Async XLA Ops:
  7.2 199.0 %copy-start = (bf16[512,1024]{1,0:T(8,128)(2,1)S(1)}, bf16[512,1024]{1,0:T(8,128)(2,1)}, u32[]{:S(2)}) copy-start(bf16[512,1024]{1,0:T(8,128)(2,1)} %param.33) | copy-start | bytes 3145732
  7.2 9.7 copy-start.5
  7.2 174.5 %all-gather.5.cloned.1.call-start = ((), (), s32[]{:S(2)}) async-start(), calls=%async_computation.3 | async-start | bytes 2359296 | tf_op jit(solution)/shard_map/all_gather | solution.py:286
  9.3 7.6 copy-start.93
  18.4 43.0 %copy-start.55 = (f32[2,128]{1,0:T(2,128)}, f32[2,128]{1,0:T(2,128)S(1)}, u32[]{:S(2)}) copy-start(f32[2,128]{1,0:T(2,128)S(1)} %add_rsqrt_fusion.4) | copy-start | bytes 3076
  19.2 42.3 %copy-start.25 = (bf16[2,128,512]{2,1,0:T(8,128)(2,1)}, bf16[2,128,512]{2,1,0:T(8,128)(2,1)S(1)}, u32[]{:S(2)}) copy-start(bf16[2,128,512]{2,1,0:T(8,128)(2,1)S(1)} %add_convert_fusion.5) | copy-start | bytes 786436
  21.4 173.7 %all-gather.3.cloned.1.call-start = ((), (), s32[]{:S(2)}) async-start(), calls=%async_computation.2 | async-start | bytes 2359296 | tf_op jit(solution)/shard_map/all_gather | solution.py:287
  23.5 511.8 %reduce-scatter.3.cloned.1.call-start = ((), (), s32[]{:S(2)}) async-start(), calls=%async_computation.4 | async-start | bytes 2359296 | tf_op jit(solution)/shard_map/reduce_scatter | solution.py:437
  65.2 9.4 copy-start.17
  116.8 63.9 %copy-start.53 = (bf16[2,128,512]{2,1,0:T(8,128)(2,1)S(1)}, bf16[2,128,512]{2,1,0:T(8,128)(2,1)}, u32[]{:S(2)}) copy-start(bf16[2,128,512]{2,1,0:T(8,128)(2,1)} %get-tuple-element.199) | copy-start | bytes 786436
  116.8 64.1 %copy-start.82 = (bf16[1024]{0:T(1024)(128)(2,1)S(1)}, bf16[1024]{0:T(1024)(128)(2,1)}, u32[]{:S(2)}) copy-start(bf16[1024]{0:T(1024)(128)(2,1)} %param.34) | copy-start | bytes 6148
  116.8 64.1 %copy-start.78 = (s32[2]{0:T(128)S(1)}, s32[2]{0:T(128)}, u32[]{:S(2)}) copy-start(s32[2]{0:T(128)} %param.22) | copy-start | bytes 28
  116.8 64.3 %copy-start.76 = (bf16[2,512]{1,0:T(2,128)(2,1)S(1)}, bf16[2,512]{1,0:T(2,128)(2,1)}, u32[]{:S(2)}) copy-start(bf16[2,512]{1,0:T(2,128)(2,1)} %param.36) | copy-start | bytes 6148
  116.9 64.9 %copy-start.54 = (bf16[512,9]{0,1:T(8,128)(2,1)S(1)}, bf16[512,9]{0,1:T(8,128)(2,1)}, u32[]{:S(2)}) copy-start(bf16[512,9]{0,1:T(8,128)(2,1)} %param.35) | copy-start | bytes 27652
  180.9 8.8 copy-start.30
  181.0 8.8 copy-start.85
  199.0 6.0 copy-start.8
  199.0 6.0 copy-start.42
  204.9 9.1 copy-start.79
  205.0 9.1 copy-start.86
  205.0 9.8 copy-start.80
  205.0 10.4 copy-start.92
  205.6 104.4 %copy-start.57 = (f32[2,128]{1,0:T(2,128)}, f32[2,128]{1,0:T(2,128)S(1)}, u32[]{:S(2)}) copy-start(f32[2,128]{1,0:T(2,128)S(1)} %add_rsqrt_fusion.3) | copy-start | bytes 3076
  207.9 8.0 collective-permute-start
  212.8 5.5 collective-permute-start.1
  308.0 11.2 copy-start.61
  310.1 7.4 copy-start.14
  320.0 58.0 %copy-start.58 = (f32[2,128]{1,0:T(2,128)S(1)}, f32[2,128]{1,0:T(2,128)}, u32[]{:S(2)}) copy-start(f32[2,128]{1,0:T(2,128)} %copy-done.57) | copy-start | bytes 3076
  364.5 13.5 %copy-start.11 = (f32[2,128,512]{2,1,0:T(8,128)S(1)}, f32[2,128,512]{2,1,0:T(8,128)}, u32[]{:S(2)}) copy-start(f32[2,128,512]{2,1,0:T(8,128)} %copy-done.10) | copy-start | bytes 1572868
  364.6 14.7 %copy-start.45 = (f32[2,128,512]{2,1,0:T(8,128)S(1)}, f32[2,128,512]{2,1,0:T(8,128)}, u32[]{:S(2)}) copy-start(f32[2,128,512]{2,1,0:T(8,128)} %copy-done.44) | copy-start | bytes 1572868
  367.3 6.2 collective-permute-start.2
  368.6 6.2 collective-permute-start.3
  373.5 6.0 copy-start.43
  380.0 13.9 %copy-start.31 = (bf16[2,128,512]{1,2,0:T(8,128)(2,1)S(1)}, bf16[2,128,512]{1,2,0:T(8,128)(2,1)}, u32[]{:S(2)}) copy-start(bf16[2,128,512]{1,2,0:T(8,128)(2,1)} %copy-done.30) | copy-start | bytes 786436
  402.1 139.6 %reduce-scatter.5.cloned.1.call-start = ((), (), s32[]{:S(2)}) async-start(), calls=%async_computation.5 | async-start | bytes 2359296 | tf_op jit(solution)/shard_map/reduce_scatter | solution.py:440
  408.5 6.3 copy-start.72
  408.6 6.3 copy-start.73
  408.6 6.3 copy-start.62
  412.6 866.7 %all-reduce.9.cloned.1.call-start = ((), (), s32[]{:S(2)}) async-start(), calls=%async_computation.6 | async-start | bytes 25243648
  518.1 7.4 copy-start.12
  525.5 6.2 slice-start
  532.6 9.2 copy-start.9
  532.6 9.2 copy-start.56
  564.4 9.1 copy-start.3
  584.6 7.3 slice-start.2
  584.6 8.8 slice-start.3
  598.2 6.1 copy-start.16
  1316.7 13.2 copy-start.1
  (62 other events, 212.7 us)
Sparse Core Ops, SparseCore 0:
  21.5 51.9 all-gather.4
  76.3 47.7 all-gather.2
  402.2 69.2 reduce-scatter.2
  474.9 66.7 reduce-scatter.4
  1048.3 231.0 all-reduce.8
where the time goes:
time: 1360 us; the launch traced here: 1340 us
  blocking collectives  530 us (39%)
  local copies, waits for them, and re-layouts  360 us (26%)
  waiting for transfers between devices  237 us (17%)
  matrix products  103 us (8%)
  other arithmetic  76.4 us (6%)
  between operations  17.6 us (1%)
    unnamed x1, blocking collectives  407 us
    unnamed x6, waiting for transfers between devices  229 us
    unnamed x229, local copies, waits for them, and re-layouts  97.9 us
    rev x1, local copies, waits for them, and re-layouts, block_scores(): placed = skew(before_skewing, key_count)[:, :, ::-1]  63.9 us
    rev x1, local copies, waits for them, and re-layouts, attend_block_back(): grad_scores[:, :, ::-1]  60.1 us
    psum x1, blocking collectives, shards(): lax.psum((jnp.sum(convolved * mask_cols, axis=(0, 1)), mask_total), ('utt...  41.7 us
    psum x1, blocking collectives, shards(): lax.psum((jnp.sum(grad_batch, axis=(0, 1)), jnp.sum(grad_batch * normed_b...  41.2 us
    psum x1, blocking collectives, shards(): lax.psum(jnp.sum(centered * centered * mask_cols, axis=(0, 1)), ('utt', '...  39.8 us
  transfers between devices with their start and end apart: 9, of which 4 were waited for; matrix products, arithmetic and copies ran while one was open for 23% of the time, Pallas kernels for 0%

commit v1 on v0

v1 whole, which is shorter than its diff:
```python
import math

import jax
import jax.numpy as jnp
from jax import lax
from jax.sharding import PartitionSpec as P

HEADS = 8
KERNEL = 9
HEAD_DIM = 64


TOP_PRECISION = lax.Precision.HIGHEST
EPSILON = 1e-05


def with_halo(cells, sides, width):
    for axis, dim in sides:
        count = lax.axis_size(axis)
        ends = count - 1
        head = lax.slice_in_dim(cells, 0, width, axis=dim)
        tail = lax.slice_in_dim(cells, cells.shape[dim] - width, cells.shape[dim], axis=dim)
        cells = jnp.concatenate(
            [
                lax.ppermute(tail, axis, [(i, (i + 1) % count) for i in range(ends)]),
                cells,
                lax.ppermute(head, axis, [((i + 1) % count, i) for i in range(ends)]),
            ],
            axis=dim,
        )
    return cells


def project(first_operand, second_operand):
    return jnp.dot(first_operand, second_operand, preferred_element_type=jnp.float32)


def outer_sum(first_operand, second_operand):
    return jnp.einsum(
        "ufd,ufe->de", first_operand, second_operand, preferred_element_type=jnp.float32
    )


def project_back(grad_rows, weight):
    return jnp.einsum("ufe,de->ufd", grad_rows, weight, preferred_element_type=jnp.float32)


def column_sum(grad_rows):
    return jnp.sum(grad_rows.astype(jnp.float32), axis=(0, 1))


def flatten_grads(members):
    flattened = jnp.concatenate([member.reshape(-1) for member in members])
    return flattened


def restore_grads(flattened, members):
    restored = []
    offset = 0
    for member in members:
        element_count = member.size
        restored.append(flattened[offset : offset + element_count].reshape(member.shape))
        offset = offset + element_count
    return tuple(restored)


def norm_forward(values, gain_vector, shift_vector):
    average = jnp.mean(values, axis=-1, keepdims=True)
    centered = values - average
    spread = jnp.mean(centered * centered, axis=-1, keepdims=True)
    inverse = lax.rsqrt(spread + EPSILON)
    normed = centered * inverse
    return (
        normed * gain_vector.astype(jnp.float32) + shift_vector.astype(jnp.float32),
        normed,
        inverse,
    )


def norm_backward(grad_rows, normed, inverse, gain_vector):
    scaled = grad_rows * gain_vector.astype(jnp.float32)
    row_inner = (
        scaled
        - jnp.mean(scaled, axis=-1, keepdims=True)
        - normed * jnp.mean(scaled * normed, axis=-1, keepdims=True)
    )
    return (
        row_inner * inverse,
        jnp.sum(grad_rows * normed, axis=(0, 1)),
        jnp.sum(grad_rows, axis=(0, 1)),
    )


def silu_slope(preact):
    logistic = jax.nn.sigmoid(preact)
    return logistic * (1.0 + preact * (1.0 - logistic))


def feed_forward(values, gain_vector, shift_vector, weight_in, bias_in, weight_out, bias_out):
    normed_out, normed, inverse = norm_forward(values, gain_vector, shift_vector)
    hidden = normed_out.astype(jnp.bfloat16)
    preact = project(hidden, weight_in) + bias_in.astype(jnp.float32)
    active = jax.nn.silu(preact).astype(jnp.bfloat16)
    return (
        project(active, weight_out) + bias_out.astype(jnp.float32),
        (normed, inverse, hidden, preact, active),
    )


def feed_backward(grad_rows, stored, gain_vector, weight_in, weight_out):
    normed, inverse, hidden, preact, active = stored
    grad_low = grad_rows.astype(jnp.bfloat16)
    grad_weight_out = outer_sum(active, grad_low)
    grad_bias_out = column_sum(grad_low)
    grad_pre = (project_back(grad_low, weight_out) * silu_slope(preact)).astype(jnp.bfloat16)
    grad_weight_in = outer_sum(hidden, grad_pre)
    grad_bias_in = column_sum(grad_pre)
    grad_values, grad_gain, grad_shift = norm_backward(
        project_back(grad_pre, weight_in), normed, inverse, gain_vector
    )
    return (
        grad_values,
        grad_gain,
        grad_shift,
        grad_weight_in,
        grad_bias_in,
        grad_weight_out,
        grad_bias_out,
    )


def axis_bits(axis):
    return [(axis, 1 << bit) for bit in range(lax.axis_size(axis).bit_length() - 1)]


def swap(values, step):
    axis, mask = step
    return lax.ppermute(values, axis, [(i, i ^ mask) for i in range(lax.axis_size(axis))])


def side(step):
    axis, mask = step
    return (lax.axis_index(axis) // mask) % 2


def scatter_rows(rows, steps):
    for step in steps:
        half = rows.shape[0] // 2
        mine = side(step)
        sent = lax.dynamic_slice_in_dim(rows, (1 - mine) * half, half, 0)
        kept = lax.dynamic_slice_in_dim(rows, mine * half, half, 0)
        rows = (kept.astype(jnp.float32) + swap(sent, step).astype(jnp.float32)).astype(
            jnp.bfloat16
        )
    return rows


def gather_rows(rows, steps):
    for step in reversed(steps):
        other = swap(rows, step)
        first = side(step) == 0
        rows = jnp.concatenate(
            [jnp.where(first, rows, other), jnp.where(first, other, rows)], axis=0
        )
    return rows


def step_orders():
    utt, seq = axis_bits("utt"), axis_bits("seq")
    near, across, line = utt[:1], utt[1:], seq[:1]
    rest = seq[1:]
    return (
        near + line + across + rest,
        near + across + line + rest,
        near + rest + line + across,
    )


def all_shared(rows):
    count = lax.axis_size("utt") * lax.axis_size("seq")
    copies = jnp.broadcast_to(rows[None], (count,) + rows.shape)
    return lax.all_to_all(copies, ("utt", "seq"), 0, 0, tiled=True)


def as_rows(members):
    pieces = []
    for member in members:
        for start in range(0, member.shape[1], 512):
            pieces.append(member[:, start : start + 512].astype(jnp.bfloat16))
    return jnp.concatenate(pieces, axis=0)


def from_rows(rows, shapes):
    restored = []
    offset = 0
    for height, width in shapes:
        columns = []
        for _ in range(width // 512):
            columns.append(rows[offset : offset + height])
            offset += height
        restored.append(jnp.concatenate(columns, axis=1).astype(jnp.float32))
    return restored


def angle_tables(frame_count, features):
    halves = jnp.arange(features // 2, dtype=jnp.int32).astype(jnp.float32)
    frequencies = jnp.exp(halves * (-2.0 * math.log(10000.0) / features))
    fine = 32
    low_angles = jnp.arange(fine, dtype=jnp.int32).astype(jnp.float32)[:, None] * frequencies
    high_angles = (fine * jnp.arange(frame_count // fine, dtype=jnp.int32)).astype(jnp.float32)[
        :, None
    ] * frequencies
    low_sin, low_cos = jnp.sin(low_angles)[None], jnp.cos(low_angles)[None]
    high_sin, high_cos = jnp.sin(high_angles)[:, None], jnp.cos(high_angles)[:, None]
    sines = high_sin * low_cos + high_cos * low_sin
    cosines = high_cos * low_cos - high_sin * low_sin
    shape = (frame_count, features // 2)
    return sines.reshape(shape), cosines.reshape(shape)


def heads_out(blocks, groups):
    return lax.all_to_all(jnp.tile(blocks, (groups, 1, 1)), "seq", 0, 0, tiled=True)


def shards(
    frames,
    lengths,
    out_grad,
    norm_gain,
    norm_bias,
    feed_in,
    feed_in_bias,
    feed_out,
    feed_out_bias,
    attend_in,
    attend_vectors,
    attend_out,
    mixer_in,
    mixer_in_bias,
    depthwise,
    mixer_vectors,
    mixer_out,
    batch_gain,
    batch_shift,
    running_mean,
    running_variance,
):
    utt_rows, block_frames, features = frames.shape
    seq_count = lax.axis_size("seq")
    seq_index = lax.axis_index("seq")
    count = lax.axis_size("utt") * seq_count
    frames_all = block_frames * seq_count
    groups = seq_count // HEADS
    head, group = seq_index % HEADS, seq_index // HEADS
    query_frames = frames_all // groups
    first_frame = seq_index * block_frames
    frame_mask = (
        (first_frame + jnp.arange(block_frames, dtype=jnp.int32))[None, :] < lengths[:, None]
    ).astype(jnp.float32)
    mask_cols = frame_mask[..., None]
    first_out, first_stored = feed_forward(
        frames,
        norm_gain[0],
        norm_bias[0],
        feed_in[0],
        feed_in_bias[0],
        feed_out[0],
        feed_out_bias[0],
    )
    after_first = frames + 0.5 * first_out
    attend_normed, normed_two, inverse_two = norm_forward(after_first, norm_gain[1], norm_bias[1])
    hidden_two = attend_normed.astype(jnp.bfloat16)
    queries = project(hidden_two, attend_in[0]) + attend_vectors[0].astype(jnp.float32)
    key_rows = project(hidden_two, attend_in[1]).astype(jnp.bfloat16)
    value_rows = (project(hidden_two, attend_in[2]) + attend_vectors[1].astype(jnp.float32)).astype(
        jnp.bfloat16
    )
    content = (queries + attend_vectors[3].astype(jnp.float32)).astype(jnp.bfloat16)
    sent = jnp.stack([content, key_rows, value_rows], axis=2).reshape(
        utt_rows, block_frames, 3, HEADS, HEAD_DIM
    )
    sent = jnp.transpose(sent, (3, 1, 0, 2, 4)).reshape(
        HEADS, block_frames, utt_rows * 3 * HEAD_DIM
    )
    arrived = heads_out(sent, groups).reshape(frames_all, utt_rows, 3, HEAD_DIM)
    start_query = group * query_frames
    head_content = lax.dynamic_slice_in_dim(arrived[:, :, 0], start_query, query_frames, 0)
    head_keys, head_values = arrived[:, :, 1], arrived[:, :, 2]
    head_vectors = lax.dynamic_slice_in_dim(
        attend_vectors.astype(jnp.float32), head * HEAD_DIM, HEAD_DIM, 1
    )
    head_offset = (
        head_content.astype(jnp.float32) + (head_vectors[4] - head_vectors[3])
    ).astype(jnp.bfloat16)
    head_weight = lax.dynamic_slice_in_dim(attend_in[3], head * HEAD_DIM, HEAD_DIM, 1).reshape(
        features // 2, 2, HEAD_DIM
    )
    sin_weight, cos_weight = head_weight[:, 0], head_weight[:, 1]
    sines, cosines = angle_tables(frames_all, features)
    key_table = jnp.concatenate([cosines, sines], axis=1).astype(jnp.bfloat16)
    query_sin = lax.dynamic_slice_in_dim(sines, start_query, query_frames, 0)[:, None]
    query_cos = lax.dynamic_slice_in_dim(cosines, start_query, query_frames, 0)[:, None]

    def turn(sin_part, cos_part):
        return jnp.concatenate(
            [
                sin_part * query_sin + cos_part * query_cos,
                cos_part * query_sin - sin_part * query_cos,
            ],
            axis=-1,
        ).astype(jnp.bfloat16)

    def contract(spec, first_operand, second_operand):
        return jnp.einsum(spec, first_operand, second_operand, preferred_element_type=jnp.float32)

    turned = turn(
        contract("qud,id->qui", head_offset, sin_weight),
        contract("qud,id->qui", head_offset, cos_weight),
    )
    scores = (
        contract("qud,kud->uqk", head_content, head_keys)
        + contract("qui,ki->uqk", turned, key_table)
    ) * HEAD_DIM ** (-0.5)
    allowed = jnp.arange(frames_all, dtype=jnp.int32)[None, None, :] < lengths[:, None, None]
    scores = jnp.where(allowed, scores, -1000000000.0)
    shifted = jnp.exp(scores - jnp.max(scores, axis=-1, keepdims=True))
    weights = (shifted / jnp.sum(shifted, axis=-1, keepdims=True)).astype(jnp.bfloat16)
    head_attended = contract("uqk,kud->qud", weights, head_values).astype(jnp.bfloat16)

    def frames_back(rows):
        width = rows.shape[-1]
        rows = rows.reshape(1, HEADS, block_frames, width)
        if groups > 1:
            rows = lax.dynamic_update_slice_in_dim(
                jnp.zeros((groups,) + rows.shape[1:], rows.dtype), rows, group, 0
            )
        rows = lax.all_to_all(
            rows.reshape(seq_count, block_frames, width), "seq", 0, 0, tiled=True
        ).reshape(groups, HEADS, block_frames, width)
        return lax.dynamic_slice_in_dim(rows, group, 1, 0)[0]

    def join_heads(blocks):
        blocks = blocks.reshape(HEADS, block_frames, utt_rows, HEAD_DIM)
        return jnp.transpose(blocks, (2, 1, 0, 3)).reshape(utt_rows, block_frames, features)

    attended_low = join_heads(
        frames_back(head_attended.reshape(query_frames, utt_rows * HEAD_DIM))
    )
    after_attend = (
        after_first + project(attended_low, attend_out) + attend_vectors[2].astype(jnp.float32)
    )
    mixer_normed, normed_three, inverse_three = norm_forward(
        after_attend, norm_gain[2], norm_bias[2]
    )
    hidden_three = mixer_normed.astype(jnp.bfloat16)
    mixer_pre = project(hidden_three, mixer_in) + mixer_in_bias.astype(jnp.float32)
    linear_half = mixer_pre[..., :features]
    gate_half = jax.nn.sigmoid(mixer_pre[..., features:])
    gated_units = (linear_half * gate_half * mask_cols).astype(jnp.bfloat16)
    margin = KERNEL // 2
    widened = with_halo(gated_units, (("seq", 1),), margin)
    kernel_rows = depthwise.astype(jnp.float32)
    convolved = mixer_vectors[0].astype(jnp.float32) + sum(
        (
            kernel_rows[:, offset] * widened[:, offset : offset + block_frames].astype(jnp.float32)
            for offset in range(KERNEL)
        )
    )
    mask_total = jnp.sum(frame_mask)
    local_sum = jnp.sum(convolved * mask_cols, axis=(0, 1))
    local_average = local_sum / jnp.maximum(mask_total, 1.0)
    local_centered = (convolved - local_average) * mask_cols
    local_square = jnp.sum(local_centered * local_centered, axis=(0, 1))
    shared = all_shared(
        jnp.stack([local_sum, local_square, jnp.full_like(local_sum, mask_total), local_average])
    )
    valid_count = jnp.sum(shared[:, 2], axis=0)
    average = jnp.sum(shared[:, 0], axis=0) / valid_count
    drift = shared[:, 3] - average
    variance = jnp.sum(shared[:, 1] + shared[:, 2] * drift * drift, axis=0) / valid_count
    centered = convolved - average
    inverse_batch = lax.rsqrt(variance + EPSILON)
    normed_batch = centered * inverse_batch
    batch_out = normed_batch * batch_gain.astype(jnp.float32) + batch_shift.astype(jnp.float32)
    swished = jax.nn.silu(batch_out).astype(jnp.bfloat16)
    after_mixer = after_attend + project(swished, mixer_out) + mixer_vectors[1].astype(jnp.float32)
    second_out, second_stored = feed_forward(
        after_mixer,
        norm_gain[3],
        norm_bias[3],
        feed_in[1],
        feed_in_bias[1],
        feed_out[1],
        feed_out_bias[1],
    )
    after_second = after_mixer + 0.5 * second_out
    layer_output, normed_last, inverse_last = norm_forward(after_second, norm_gain[4], norm_bias[4])
    grad_second, gain_last, shift_last = norm_backward(
        out_grad, normed_last, inverse_last, norm_gain[4]
    )
    second_back = feed_backward(
        0.5 * grad_second, second_stored, norm_gain[3], feed_in[1], feed_out[1]
    )
    second_rows = lax.psum(as_rows([second_back[3], second_back[5]]), ("utt", "seq"))
    grad_mixer = grad_second + second_back[0]
    grad_branch = grad_mixer.astype(jnp.bfloat16)
    mixer_out_grad = outer_sum(swished, grad_branch)
    out_bias_grad = column_sum(grad_branch)
    grad_batch = project_back(grad_branch, mixer_out) * silu_slope(batch_out)
    batch_shift_grad, batch_gain_grad = jnp.sum(
        all_shared(
            jnp.stack(
                [jnp.sum(grad_batch, axis=(0, 1)), jnp.sum(grad_batch * normed_batch, axis=(0, 1))]
            )
        ),
        axis=0,
    )
    grad_conv = (
        batch_gain.astype(jnp.float32)
        * inverse_batch
        * (
            grad_batch
            - mask_cols / valid_count * (batch_shift_grad + normed_batch * batch_gain_grad)
        )
    ).astype(jnp.bfloat16)
    grad_wide = with_halo(grad_conv, (("seq", 1),), margin)
    grad_gated = mask_cols * sum(
        (
            kernel_rows[:, offset]
            * grad_wide[:, 2 * margin - offset : 2 * margin - offset + block_frames].astype(
                jnp.float32
            )
            for offset in range(KERNEL)
        )
    )
    grad_conv_wide = grad_conv.astype(jnp.float32)
    depthwise_grad = jnp.stack(
        [
            jnp.sum(
                grad_conv_wide * widened[:, offset : offset + block_frames].astype(jnp.float32),
                axis=(0, 1),
            )
            for offset in range(KERNEL)
        ],
        axis=1,
    )
    kernel_bias_grad = column_sum(grad_conv)
    grad_mixer_pre = jnp.concatenate(
        [grad_gated * gate_half, grad_gated * linear_half * gate_half * (1.0 - gate_half)], axis=-1
    ).astype(jnp.bfloat16)
    mixer_in_grad = outer_sum(hidden_three, grad_mixer_pre)
    mixer_in_bias_grad = column_sum(grad_mixer_pre)
    grad_three, gain_three, shift_three = norm_backward(
        project_back(grad_mixer_pre, mixer_in), normed_three, inverse_three, norm_gain[2]
    )
    grad_attend = grad_mixer + grad_three
    mixer_vectors_grad = jnp.stack([kernel_bias_grad, out_bias_grad])
    grad_branch_two = grad_attend.astype(jnp.bfloat16)
    attend_out_grad = outer_sum(attended_low, grad_branch_two)
    out_bias_two = column_sum(grad_branch_two)
    mixer_rows = lax.psum(
        as_rows([mixer_out_grad, mixer_in_grad, attend_out_grad]), ("utt", "seq")
    )
    grad_attended = project_back(grad_branch_two, attend_out).astype(jnp.bfloat16)
    grad_blocks = grad_attended.reshape(utt_rows, block_frames, HEADS, HEAD_DIM)
    grad_blocks = jnp.transpose(grad_blocks, (2, 1, 0, 3)).reshape(
        HEADS, block_frames, utt_rows * HEAD_DIM
    )
    head_grad = lax.dynamic_slice_in_dim(
        heads_out(grad_blocks, groups).reshape(frames_all, utt_rows, HEAD_DIM),
        start_query,
        query_frames,
        0,
    )
    grad_weights = contract("qud,kud->uqk", head_grad, head_values)
    wide = weights.astype(jnp.float32)
    row_inner = jnp.sum(wide * grad_weights, axis=-1, keepdims=True)
    grad_scores = (wide * (grad_weights - row_inner) * HEAD_DIM ** (-0.5)).astype(jnp.bfloat16)
    head_grad_values = contract("uqk,qud->kud", weights, head_grad)
    head_grad_keys = contract("uqk,qud->kud", grad_scores, head_content)
    head_grad_content = contract("uqk,kud->qud", grad_scores, head_keys)
    grad_turned = contract("uqk,ki->qui", grad_scores, key_table)
    half_features = features // 2
    grad_sin = grad_turned[..., :half_features]
    grad_cos = grad_turned[..., half_features:]
    from_sin = (grad_sin * query_sin - grad_cos * query_cos).astype(jnp.bfloat16)
    from_cos = (grad_sin * query_cos + grad_cos * query_sin).astype(jnp.bfloat16)
    head_grad_position = contract("qui,id->qud", from_sin, sin_weight) + contract(
        "qui,id->qud", from_cos, cos_weight
    )
    head_weight_grad = jnp.stack(
        [
            contract("qui,qud->id", from_sin, head_offset),
            contract("qui,qud->id", from_cos, head_offset),
        ],
        axis=1,
    ).reshape(features, HEAD_DIM)
    position_weight_grad = lax.dynamic_update_slice_in_dim(
        jnp.zeros((features, features), jnp.float32), head_weight_grad, head * HEAD_DIM, 1
    )
    head_vector_grads = lax.dynamic_update_slice_in_dim(
        jnp.zeros((2, features), jnp.float32),
        jnp.stack([jnp.sum(head_grad_content, axis=(0, 1)), jnp.sum(head_grad_position, axis=(0, 1))]),
        head * HEAD_DIM,
        1,
    )
    head_grad_query = (head_grad_content + head_grad_position).astype(jnp.bfloat16)
    if groups == 1:
        returned = lax.all_to_all(
            jnp.stack(
                [
                    head_grad_query,
                    head_grad_keys.astype(jnp.bfloat16),
                    head_grad_values.astype(jnp.bfloat16),
                ],
                axis=2,
            ).reshape(seq_count, block_frames, utt_rows * 3 * HEAD_DIM),
            "seq",
            0,
            0,
            tiled=True,
        ).reshape(HEADS, block_frames, utt_rows, 3, HEAD_DIM)
        query_low, key_low, value_low = (join_heads(returned[:, :, :, i]) for i in range(3))
    else:
        query_low = join_heads(
            frames_back(head_grad_query.reshape(query_frames, utt_rows * HEAD_DIM))
        )
        returned = lax.all_to_all(
            jnp.stack([head_grad_keys, head_grad_values], axis=2)
            .astype(jnp.bfloat16)
            .reshape(seq_count, block_frames, utt_rows * 2 * HEAD_DIM),
            "seq",
            0,
            0,
            tiled=True,
        )
        returned = jnp.sum(
            returned.astype(jnp.float32).reshape(
                groups, HEADS, block_frames, utt_rows, 2, HEAD_DIM
            ),
            axis=0,
        ).astype(jnp.bfloat16)
        key_low, value_low = (join_heads(returned[:, :, :, i]) for i in range(2))
    attend_in_grads = [
        outer_sum(hidden_two, query_low),
        outer_sum(hidden_two, key_low),
        outer_sum(hidden_two, value_low),
    ]
    attend_vector_parts = [
        column_sum(query_low)[None],
        column_sum(value_low)[None],
        out_bias_two[None],
        head_vector_grads,
    ]
    grad_hidden = (
        project_back(query_low, attend_in[0])
        + project_back(key_low, attend_in[1])
        + project_back(value_low, attend_in[2])
    )
    grad_two, gain_two, shift_two = norm_backward(
        grad_hidden, normed_two, inverse_two, norm_gain[1]
    )
    grad_first = grad_attend + grad_two
    first_back = feed_backward(
        0.5 * grad_first, first_stored, norm_gain[0], feed_in[0], feed_out[0]
    )
    frames_grad = grad_first + first_back[0]
    norm_gain_grad = jnp.stack([first_back[1], gain_two, gain_three, second_back[1], gain_last])
    norm_bias_grad = jnp.stack([first_back[2], shift_two, shift_three, second_back[2], shift_last])
    feed_in_bias_grad = jnp.stack([first_back[4], second_back[4]])
    feed_out_bias_grad = jnp.stack([first_back[6], second_back[6]])
    attend_vectors_grad = jnp.concatenate(attend_vector_parts, axis=0)
    vectors = (
        norm_gain_grad,
        norm_bias_grad,
        feed_in_bias_grad,
        feed_out_bias_grad,
        attend_vectors_grad,
        mixer_in_bias_grad,
        depthwise_grad,
        mixer_vectors_grad,
    )
    flat = flatten_grads(vectors)
    vector_rows = -(-flat.shape[0] // (512 * count)) * count
    flat = jnp.pad(flat, (0, vector_rows * 512 - flat.shape[0]))
    last = as_rows([first_back[3], first_back[5]])
    middle = as_rows(attend_in_grads + [position_weight_grad])
    cuts = (3 * 512, 6 * 512)
    stripes = (
        jnp.concatenate([last[: cuts[0]], middle[:768]], axis=0),
        jnp.concatenate([last[cuts[0] : cuts[1]], middle[768:1536]], axis=0),
        jnp.concatenate(
            [last[cuts[1] :], middle[1536:], flat.astype(jnp.bfloat16).reshape(-1, 512)], axis=0
        ),
    )
    gathered = [
        gather_rows(scatter_rows(stripe, order), order)
        for stripe, order in zip(stripes, step_orders())
    ]
    last = jnp.concatenate([gathered[0][:1536], gathered[1][:1536], gathered[2][:1024]], axis=0)
    middle = jnp.concatenate(
        [gathered[0][1536:], gathered[1][1536:], gathered[2][1024:1536]], axis=0
    )
    vectors = restore_grads(
        gathered[2][1536:].astype(jnp.float32).reshape(-1), vectors
    )
    (
        norm_gain_grad,
        norm_bias_grad,
        feed_in_bias_grad,
        feed_out_bias_grad,
        attend_vectors_grad,
        mixer_in_bias_grad,
        depthwise_grad,
        mixer_vectors_grad,
    ) = vectors
    wide_in, wide_out = feed_in.shape[1:], feed_out.shape[1:]
    first_in, first_out_grad = from_rows(last, (wide_in, wide_out))
    second_in, second_out_grad = from_rows(second_rows, (wide_in, wide_out))
    feed_in_grad = jnp.stack([first_in, second_in])
    feed_out_grad = jnp.stack([first_out_grad, second_out_grad])
    attend_in_grad = middle.astype(jnp.float32).reshape(attend_in.shape)
    mixer_out_grad, mixer_in_grad, attend_out_grad = from_rows(
        mixer_rows, (mixer_out.shape, mixer_in.shape, attend_out.shape)
    )
    new_mean = 0.9 * running_mean + 0.1 * average
    new_variance = 0.9 * running_variance + 0.1 * variance * valid_count / (valid_count - 1.0)
    return (
        layer_output,
        frames_grad,
        norm_gain_grad,
        norm_bias_grad,
        feed_in_grad,
        feed_in_bias_grad,
        feed_out_grad,
        feed_out_bias_grad,
        attend_in_grad,
        attend_vectors_grad,
        attend_out_grad,
        mixer_in_grad,
        mixer_in_bias_grad,
        depthwise_grad,
        mixer_vectors_grad,
        mixer_out_grad,
        batch_gain_grad,
        batch_shift_grad,
        new_mean,
        new_variance,
    )


def solution(mesh):
    return jax.shard_map(
        shards,
        mesh=mesh,
        in_specs=(
            P("utt", "seq", None),
            P("utt"),
            P("utt", "seq", None),
            P(),
            P(),
            P(),
            P(),
            P(),
            P(),
            P(),
            P(),
            P(),
            P(),
            P(),
            P(),
            P(),
            P(),
            P(),
            P(),
            P(),
            P(),
        ),
        out_specs=(
            P("utt", "seq", None),
            P("utt", "seq", None),
            P(),
            P(),
            P(),
            P(),
            P(),
            P(),
            P(),
            P(),
            P(),
            P(),
            P(),
            P(),
            P(),
            P(),
            P(),
            P(),
            P(),
            P(),
        ),
        check_vma=False,
    )
```

time: 1360 us -> 524 us (0.39); the launches traced: 1340 us -> 519 us
  blocking collectives: 530 us -> 0 us
  local copies, waits for them, and re-layouts: 360 us -> 56.6 us
  starting transfers between devices: 12.6 us -> 65.1 us
  waiting for transfers between devices: 237 us -> 214 us
    unnamed x1 -> x0, blocking collectives: 407 us -> none
    unnamed x6 -> x1, waiting for transfers between devices: 229 us -> 0.02 us
    rev x4 -> x0, local copies, waits for them, and re-layouts: 126 us -> none  [the longest x1 63.9 us: block_scores(): placed = skew(before_skewing, key_count)[:, :, ::-1]]
    psum x3 -> x0, blocking collectives: 123 us -> none  [the longest x1 41.7 us: shards(): lax.psum((jnp.sum(convolved * mask_cols, axis=(0, 1)), mask_total), ('utt...]
    psum x0 -> x1, waiting for transfers between devices: none -> 95.7 us  [shards(): lax.psum(as_rows([second_back[3], second_back[5]]), ('utt', 'seq'))]
    unnamed x229 -> x300, local copies, waits for them, and re-layouts: 97.9 us -> 26.3 us
    ppermute x0 -> x30, waiting for transfers between devices: none -> 68 us  [swap(): lax.ppermute(values, axis, [(i, i ^ mask) for i in range(lax.axis_size(ax...]
    all_to_all x0 -> x6, waiting for transfers between devices: none -> 48.5 us  [the longest x2 15 us: heads_out(): lax.all_to_all(jnp.tile(blocks, (groups, 1, 1)), 'seq', 0, 0, tiled=True)]
  transfers between devices with their start and end apart: 9 -> 41, of which waited for: 4 -> 27; matrix products, arithmetic and copies ran while one was open for 23% -> 15% of each run, Pallas kernels for 0% -> 0%
where the time goes in v1:
time: 524 us; the launch traced here: 519 us
  waiting for transfers between devices  214 us (41%)
  matrix products  101 us (19%)
  starting transfers between devices  65.1 us (12%)
  other arithmetic  64.1 us (12%)
  local copies, waits for them, and re-layouts  56.6 us (11%)
  between operations  18.4 us (4%)
    psum x1, waiting for transfers between devices, shards(): lax.psum(as_rows([second_back[3], second_back[5]]), ('utt', 'seq'))  95.7 us
    ppermute x30, waiting for transfers between devices, swap(): lax.ppermute(values, axis, [(i, i ^ mask) for i in range(lax.axis_size(ax...  68 us
    dot_general x13, matrix products, contract(): jnp.einsum(spec, first_operand, second_operand, preferred_element_type=jn...  57.7 us
    unnamed x300, local copies, waits for them, and re-layouts  26.3 us
    ppermute x30, starting transfers between devices, swap(): lax.ppermute(values, axis, [(i, i ^ mask) for i in range(lax.axis_size(ax...  26 us
    dot_general x10, matrix products, outer_sum(): jnp.einsum('ufd,ufe->de', first_operand, second_operand, preferred_elemen...  16.7 us
    all_to_all x2, waiting for transfers between devices, heads_out(): lax.all_to_all(jnp.tile(blocks, (groups, 1, 1)), 'seq', 0, 0, tiled=True)  15 us
    all_to_all x1, waiting for transfers between devices, shards(): lax.all_to_all(jnp.stack([head_grad_query, head_grad_keys.astype(jnp.bflo...  14.5 us
  transfers between devices with their start and end apart: 41, of which 27 were waited for; matrix products, arithmetic and copies ran while one was open for 15% of the time, Pallas kernels for 0%

profile of v1, /device:TPU:0, one launch (start us, length us, event | category | flops | bytes accessed | tf_op | source)
XLA Modules:
  0.0 518.9 jit_solution(2113122539376817433)
XLA Ops:
  14.0 2.7 convolution_add_fusion.1
  22.6 7.5 %all-to-all-start = ((bf16[8,128,384]{1,2,0:T(8,128)(2,1)}), bf16[8,128,384]{1,2,0:T(8,128)(2,1)}, u32[]{:S(2)}, u32[]{:S(2)}) async-start(bf16[8,128,384]{1,2,0:T(8,128)(2,1)} %bitcast.23), calls=%async_computation | async-start | bytes 1572864 | tf_op jit(solution)/shard_map/all_to_all | solution.py:222
  33.5 2.6 copy.290
  40.0 10.4 %all-to-all-done = bf16[8,128,384]{1,2,0:T(8,128)(2,1)} async-done(((bf16[8,128,384]{1,2,0:T(8,128)(2,1)}), bf16[8,128,384]{1,2,0:T(8,128)(2,1)}, u32[]{:S(2)}, u32[]{:S(2)}) %all-to-all-start) | async-done | bytes 786464 | tf_op jit(solution)/shard_map/all_to_all | solution.py:222
  50.3 2.5 copy.285
  52.8 2.3 reshape.804
  58.6 5.7 %fusion.24 = f32[1024,1024,2]{1,0,2:T(8,128)} fusion(bf16[1024,2,256]{0,2,1:T(8,128)(2,1)S(1)} %get-tuple-element.200, bf16[1024,2,256]{0,2,1:T(8,128)(2,1)S(1)} %get-tuple-element.199, bf16[1024,256]{1,0:T(8,128)(2,1)S(1)} %copy-done.58, bf16[1024,256]{1,0:T(8,128)(2,1)S(1)} %copy-done.59), kind=kOutput, calls=%fused_computation.47 | convolution fusion | flops 2153775104 | bytes 11534336 | tf_op jit(solution)/shard_map/qui,ki->uqk/dot_general | solution.py:314
  64.3 7.4 %fusion.198 = (f32[2,1024]{1,0:T(2,128)S(1)}, f32[2,1024,1024]{1,2,0:T(8,128)}) fusion(f32[1024,1024,2]{1,0,2:T(8,128)} %fusion.24, pred[2,1024]{1,0:T(4,128)(4,1)S(1)} %iota_compare_fusion.2, bf16[1024,2,3,64]{0,3,2,1:T(8,128)(2,1)S(1)} %copy-done.8), kind=kOutput, calls=%fused_computation.503 | convolution fusion | flops 278922240 | bytes 17313792 | tf_op jit(solution)/shard_map/sub | solution.py:326
  71.7 4.6 divide_convert_fusion
  79.2 3.6 all-to-all-start.1
  83.0 8.9 %all-to-all-done.1 = bf16[8,128,128]{1,2,0:T(8,128)(2,1)S(1)} async-done(((bf16[8,128,128]{1,2,0:T(8,128)(2,1)}), bf16[8,128,128]{1,2,0:T(8,128)(2,1)S(1)}, u32[]{:S(2)}, u32[]{:S(2)}) %all-to-all-start.1) | async-done | bytes 262176 | tf_op jit(solution)/shard_map/all_to_all | solution.py:337
  94.7 4.5 collective-permute-start
  103.8 5.2 all-to-all-start.2
  109.4 10.2 %all-to-all-done.2 = f32[32,4,512]{2,1,0:T(4,128)} async-done(((f32[32,4,512]{2,1,0:T(4,128)}), f32[32,4,512]{2,1,0:T(4,128)}, u32[]{:S(2)}, u32[]{:S(2)}) %all-to-all-start.2) | async-done | bytes 262176 | tf_op jit(solution)/shard_map/all_to_all | solution.py:182
  134.7 2.2 bitcast_convert_fusion.1
  140.1 2.6 all-to-all-start.3
  150.4 2.2 fusion.13
  155.7 3.5 collective-permute-start.3
  160.5 2.5 fusion.51
  168.5 5.8 %all-to-all-start.4 = ((bf16[8,128,128]{1,2,0:T(8,128)(2,1)}), bf16[8,128,128]{1,2,0:T(8,128)(2,1)S(1)}, u32[]{:S(2)}, u32[]{:S(2)}) async-start(bf16[8,128,128]{1,2,0:T(8,128)(2,1)} %bitcast.79), calls=%async_computation.4 | async-start | bytes 524288 | tf_op jit(solution)/shard_map/all_to_all | solution.py:222
  175.6 2.5 bitcast_convert_fusion.4
  178.1 4.6 all-to-all-done.4
  183.0 3.6 fusion.77
  186.7 4.7 fusion.147
  191.4 10.3 %fusion.78 = bf16[1024,2,1,64]{0,3,1,2:T(8,128)(2,1)} fusion(bf16[2,1024,1024]{1,2,0:T(8,128)(2,1)} %copy-done.2, f32[2,1024,1024]{1,2,0:T(8,128)} %fusion.147, bf16[1024,2,3,64]{0,3,2,1:T(8,128)(2,1)S(1)} %copy-done.9), kind=kOutput, calls=%fused_computation.138 | convolution fusion | flops 283249664 | bytes 25690112 | tf_op jit(solution)/shard_map/uqk,qud->kud/dot_general | solution.py:314
  201.7 11.8 %fusion.204 = (bf16[64]{0:T(256)(128)(2,1)S(1)}, f32[2,64,1024]{2,1,0:T(8,128)}) fusion(bf16[2,1024,1024]{1,2,0:T(8,128)(2,1)} %copy-done.2, f32[2,1024,1024]{1,2,0:T(8,128)} %fusion.147, bf16[1024,2,3,64]{0,3,2,1:T(8,128)(2,1)S(1)} %copy-done.9), kind=kOutput, calls=%fused_computation.509 | convolution fusion | flops 283249600 | bytes 25952384 | tf_op jit(solution)/shard_map/uqk,kud->qud/dot_general | solution.py:314
  213.6 13.2 %fusion.20 = f32[1024,2,512]{0,2,1:T(8,128)} fusion(bf16[2,1024,1024]{1,2,0:T(8,128)(2,1)} %copy-done.2, f32[2,1024,1024]{1,2,0:T(8,128)} %fusion.147, bf16[1024,256]{1,0:T(8,128)(2,1)} %bitcast_convert_fusion.5, bf16[1024,256]{1,0:T(8,128)(2,1)} %bitcast_convert_fusion.6), kind=kOutput, calls=%fused_computation.41 | convolution fusion | flops 2164263936 | bytes 17825792 | tf_op jit(solution)/shard_map/uqk,ki->qui/dot_general | solution.py:314
  226.8 3.1 add_convert_fusion.2
  232.6 3.5 all-to-all-start.5
  245.8 14.5 %all-to-all-done.5 = bf16[8,128,384]{1,2,0:T(8,128)(2,1)S(1)} async-done(((bf16[8,128,384]{1,2,0:T(8,128)(2,1)}), bf16[8,128,384]{1,2,0:T(8,128)(2,1)S(1)}, u32[]{:S(2)}, u32[]{:S(2)}) %all-to-all-start.5) | async-done | bytes 786464 | tf_op jit(solution)/shard_map/all_to_all | solution.py:509
  266.5 2.1 bitcast_convert_fusion.3
  271.7 2.2 bitcast_convert_fusion.2
  286.2 7.8 %collective-permute-done.5 = bf16[400,512]{1,0:T(8,128)(2,1)S(1)} collective-permute-done((bf16[400,512]{1,0:T(8,128)(2,1)S(1)}, bf16[400,512]{1,0:T(8,128)(2,1)S(1)}, u32[]{:S(2)}, u32[]{:S(2)}) %collective-permute-start.5) | collective-permute-done | bytes 409632 | tf_op jit(solution)/shard_map/ppermute | solution.py:138
  297.2 13.1 %collective-permute-done.6 = bf16[200,512]{1,0:T(8,128)(2,1)S(1)} collective-permute-done((bf16[200,512]{1,0:T(8,128)(2,1)S(1)}, bf16[200,512]{1,0:T(8,128)(2,1)S(1)}, u32[]{:S(2)}, u32[]{:S(2)}) %collective-permute-start.6) | collective-permute-done | bytes 204832 | tf_op jit(solution)/shard_map/ppermute | solution.py:138
  311.8 95.7 %all-reduce.4.cloned.1.call-done = (bf16[4096,512]{1,0:T(8,128)(2,1)}, bf16[2048,512]{1,0:T(8,128)(2,1)}) async-done(((bf16[4096,512]{1,0:T(8,128)(2,1)}, bf16[2048,512]{1,0:T(8,128)(2,1)}), (bf16[4096,512]{1,0:T(8,128)(2,1)}, bf16[2048,512]{1,0:T(8,128)(2,1)})) %all-reduce.4.cloned.1.call-update) | async-done | bytes 6291472 | tf_op jit(solution)/shard_map/psum | solution.py:404
  407.4 3.2 slice_bitcast_fusion
  424.1 2.4 collective-permute-start.11
  438.1 8.9 %collective-permute-done.27 = bf16[144,512]{1,0:T(8,128)(2,1)S(1)} collective-permute-done((bf16[144,512]{1,0:T(8,128)(2,1)S(1)}, bf16[144,512]{1,0:T(8,128)(2,1)S(1)}, u32[]{:S(2)}, u32[]{:S(2)}) %collective-permute-start.27) | collective-permute-done | bytes 147488 | tf_op jit(solution)/shard_map/ppermute | solution.py:138
  447.2 2.2 collective-permute-done.17
  450.2 3.3 collective-permute-done.28
  459.0 2.7 collective-permute-done.19
  461.9 3.6 collective-permute-done.30
  468.8 3.6 collective-permute-done.31
  474.1 3.1 collective-permute-done.21
  480.0 7.1 %collective-permute-done.32 = bf16[576,512]{1,0:T(8,128)(2,1)S(1)} collective-permute-done((bf16[576,512]{1,0:T(8,128)(2,1)S(1)}, bf16[576,512]{1,0:T(8,128)(2,1)S(1)}, u32[]{:S(2)}, u32[]{:S(2)}) %collective-permute-start.32) | collective-permute-done | bytes 589856 | tf_op jit(solution)/shard_map/ppermute | solution.py:138
  501.2 2.6 convert.242
  503.8 3.9 maximum_convert_fusion.1
  507.8 3.9 maximum_convert_fusion
  (622 shorter events, 160.4 us)
Async XLA Ops:
  7.2 85.4 %copy-start = (bf16[512,1024]{1,0:T(8,128)(2,1)S(1)}, bf16[512,1024]{1,0:T(8,128)(2,1)}, u32[]{:S(2)}) copy-start(bf16[512,1024]{1,0:T(8,128)(2,1)} %param.33) | copy-start | bytes 3145732
  10.6 82.1 %copy-start.117 = (f32[1,512]{1,0:T(1,128)}, f32[1,512]{1,0:T(1,128)S(1)}, u32[]{:S(2)}) copy-start(f32[1,512]{1,0:T(1,128)S(1)} %get-tuple-element.288) | copy-start | bytes 6148
  11.5 81.1 %copy-start.103 = (f32[1,512]{1,0:T(1,128)}, f32[1,512]{1,0:T(1,128)S(1)}, u32[]{:S(2)}) copy-start(f32[1,512]{1,0:T(1,128)S(1)} %get-tuple-element.283) | copy-start | bytes 6148
  22.6 27.7 %all-to-all-start = ((bf16[8,128,384]{1,2,0:T(8,128)(2,1)}), bf16[8,128,384]{1,2,0:T(8,128)(2,1)}, u32[]{:S(2)}, u32[]{:S(2)}) async-start(bf16[8,128,384]{1,2,0:T(8,128)(2,1)} %bitcast.23), calls=%async_computation | async-start | bytes 1572864 | tf_op jit(solution)/shard_map/all_to_all | solution.py:222
  79.2 12.7 %all-to-all-start.1 = ((bf16[8,128,128]{1,2,0:T(8,128)(2,1)}), bf16[8,128,128]{1,2,0:T(8,128)(2,1)S(1)}, u32[]{:S(2)}, u32[]{:S(2)}) async-start(bf16[8,128,128]{1,2,0:T(8,128)(2,1)} %copy.295), calls=%async_computation.1 | async-start | bytes 524288 | tf_op jit(solution)/shard_map/all_to_all | solution.py:337
  93.2 28.1 %copy-start.126 = (f32[512]{0:T(512)S(1)}, f32[512]{0:T(512)}, u32[]{:S(2)}) copy-start(f32[512]{0:T(512)} %param.40) | copy-start | bytes 6148
  93.2 28.7 %copy-start.130 = (f32[512]{0:T(512)S(1)}, f32[512]{0:T(512)}, u32[]{:S(2)}) copy-start(f32[512]{0:T(512)} %param.41) | copy-start | bytes 6148
  93.4 7.9 %collective-permute-start.1 = (bf16[2,4,512]{2,1,0:T(4,128)(2,1)S(1)}, bf16[2,4,512]{2,1,0:T(4,128)(2,1)S(1)}, u32[]{:S(2)}, u32[]{:S(2)}) collective-permute-start(bf16[2,4,512]{2,1,0:T(4,128)(2,1)S(1)} %get-tuple-element.254), channel_id=1, source_target_pairs={{1,0},{2,1},{3,2},{4,3},{5,4},{6,5},{7,6},{9,8},{10,9},{11,10},{12... | collective-permute-start | bytes 24584 | tf_op jit(solution)/shard_map/ppermute | solution.py:27
  94.7 6.6 %collective-permute-start = (bf16[2,4,512]{2,1,0:T(4,128)(2,1)S(1)}, bf16[2,4,512]{2,1,0:T(4,128)(2,1)S(1)}, u32[]{:S(2)}, u32[]{:S(2)}) collective-permute-start(bf16[2,4,512]{2,1,0:T(4,128)(2,1)S(1)} %get-tuple-element.253), channel_id=1, source_target_pairs={{0,1},{1,2},{2,3},{3,4},{4,5},{5,6},{6,7},{8,9},{9,10},{10,11},{11... | collective-permute-start | bytes 24584 | tf_op jit(solution)/shard_map/ppermute | solution.py:25
  103.8 15.8 %all-to-all-start.2 = ((f32[32,4,512]{2,1,0:T(4,128)}), f32[32,4,512]{2,1,0:T(4,128)}, u32[]{:S(2)}, u32[]{:S(2)}) async-start(f32[32,4,512]{2,1,0:T(4,128)} %broadcast_in_dim.27), calls=%async_computation.2 | async-start | bytes 524288 | tf_op jit(solution)/shard_map/all_to_all | solution.py:182
  109.2 28.6 %copy-start.127 = (f32[512]{0:T(512)}, f32[512]{0:T(512)S(1)}, u32[]{:S(2)}) copy-start(f32[512]{0:T(512)S(1)} %convert_element_type.775) | copy-start | bytes 6148
  109.3 28.6 %copy-start.128 = (f32[512]{0:T(512)}, f32[512]{0:T(512)S(1)}, u32[]{:S(2)}) copy-start(f32[512]{0:T(512)S(1)} %convert_element_type.774) | copy-start | bytes 6148
  140.1 12.5 %all-to-all-start.3 = ((f32[32,2,512]{2,1,0:T(2,128)}), f32[32,2,512]{2,1,0:T(2,128)S(1)}, u32[]{:S(2)}, u32[]{:S(2)}) async-start(f32[32,2,512]{2,1,0:T(2,128)} %broadcast_in_dim.28), calls=%async_computation.3 | async-start | bytes 262144 | tf_op jit(solution)/shard_map/all_to_all | solution.py:182
  155.7 7.5 %collective-permute-start.3 = (bf16[2,4,512]{2,1,0:T(4,128)(2,1)S(1)}, bf16[2,4,512]{2,1,0:T(4,128)(2,1)S(1)}, u32[]{:S(2)}, u32[]{:S(2)}) collective-permute-start(bf16[2,4,512]{2,1,0:T(4,128)(2,1)S(1)} %get-tuple-element.249), channel_id=1, source_target_pairs={{0,1},{1,2},{2,3},{3,4},{4,5},{5,6},{6,7},{8,9},{9,10},{10,11},{11... | collective-permute-start | bytes 24584 | tf_op jit(solution)/shard_map/ppermute | solution.py:25
  159.2 5.5 %collective-permute-start.2 = (bf16[2,4,512]{2,1,0:T(4,128)(2,1)S(1)}, bf16[2,4,512]{2,1,0:T(4,128)(2,1)S(1)}, u32[]{:S(2)}, u32[]{:S(2)}) collective-permute-start(bf16[2,4,512]{2,1,0:T(4,128)(2,1)S(1)} %get-tuple-element.248), channel_id=1, source_target_pairs={{1,0},{2,1},{3,2},{4,3},{5,4},{6,5},{7,6},{9,8},{10,9},{11,10},{12... | collective-permute-start | bytes 24584 | tf_op jit(solution)/shard_map/ppermute | solution.py:27
  168.5 14.2 %all-to-all-start.4 = ((bf16[8,128,128]{1,2,0:T(8,128)(2,1)}), bf16[8,128,128]{1,2,0:T(8,128)(2,1)S(1)}, u32[]{:S(2)}, u32[]{:S(2)}) async-start(bf16[8,128,128]{1,2,0:T(8,128)(2,1)} %bitcast.79), calls=%async_computation.4 | async-start | bytes 524288 | tf_op jit(solution)/shard_map/all_to_all | solution.py:222
  232.6 27.7 %all-to-all-start.5 = ((bf16[8,128,384]{1,2,0:T(8,128)(2,1)}), bf16[8,128,384]{1,2,0:T(8,128)(2,1)S(1)}, u32[]{:S(2)}, u32[]{:S(2)}) async-start(bf16[8,128,384]{1,2,0:T(8,128)(2,1)} %copy.313), calls=%async_computation.5 | async-start | bytes 1572864 | tf_op jit(solution)/shard_map/all_to_all | solution.py:509
  236.1 171.3 %all-reduce.4.cloned.1.call-start = ((), (), s32[]{:S(2)}) async-start(), calls=%async_computation.6 | async-start | bytes 12582912 | tf_op jit(solution)/shard_map/psum | solution.py:404
  277.3 5.2 collective-permute-start.4
  280.5 2.9 collective-permute-start.24
  280.7 14.0 %collective-permute-start.14 = (bf16[1152,512]{1,0:T(8,128)(2,1)S(1)}, bf16[1152,512]{1,0:T(8,128)(2,1)S(1)}, u32[]{:S(2)}, u32[]{:S(2)}) collective-permute-start(bf16[1152,512]{1,0:T(8,128)(2,1)S(1)} %constant_dynamic-slice_fusion.9), channel_id=1, source_target_pairs={{0,8},{8,0},{16,24},{24,16},{1,9},{9,1},{17,25},{25,17},{2,10},{10... | collective-permute-start | bytes 3538952 | tf_op jit(solution)/shard_map/ppermute | solution.py:138
  282.8 11.3 %collective-permute-start.5 = (bf16[400,512]{1,0:T(8,128)(2,1)S(1)}, bf16[400,512]{1,0:T(8,128)(2,1)S(1)}, u32[]{:S(2)}, u32[]{:S(2)}) collective-permute-start(bf16[400,512]{1,0:T(8,128)(2,1)S(1)} %constant_dynamic-slice_fusion.13), channel_id=1, source_target_pairs={{0,2},{1,3},{2,0},{3,1},{4,6},{5,7},{6,4},{7,5},{8,10},{9,11},{10,... | collective-permute-start | bytes 1228808 | tf_op jit(solution)/shard_map/ppermute | solution.py:138
  284.7 141.8 %collective-permute-start.25 = (bf16[576,512]{1,0:T(8,128)(2,1)}, bf16[576,512]{1,0:T(8,128)(2,1)}, u32[]{:S(2)}, u32[]{:S(2)}) collective-permute-start(bf16[576,512]{1,0:T(8,128)(2,1)} %constant_dynamic-slice_fusion.3), channel_id=1, source_target_pairs={{0,16},{8,24},{16,0},{24,8},{1,17},{9,25},{17,1},{25,9},{2,18},{10... | collective-permute-start | bytes 1769480 | tf_op jit(solution)/shard_map/ppermute | solution.py:138
  294.2 16.1 %collective-permute-start.6 = (bf16[200,512]{1,0:T(8,128)(2,1)S(1)}, bf16[200,512]{1,0:T(8,128)(2,1)S(1)}, u32[]{:S(2)}, u32[]{:S(2)}) collective-permute-start(bf16[200,512]{1,0:T(8,128)(2,1)S(1)} %constant_dynamic-slice_fusion.12), channel_id=1, source_target_pairs={{0,4},{1,5},{2,6},{3,7},{4,0},{5,1},{6,2},{7,3},{8,12},{9,13},{10,... | collective-permute-start | bytes 614408 | tf_op jit(solution)/shard_map/ppermute | solution.py:138
  295.9 133.3 %collective-permute-start.15 = (bf16[576,512]{1,0:T(8,128)(2,1)}, bf16[576,512]{1,0:T(8,128)(2,1)}, u32[]{:S(2)}, u32[]{:S(2)}) collective-permute-start(bf16[576,512]{1,0:T(8,128)(2,1)} %constant_dynamic-slice_fusion.8), channel_id=1, source_target_pairs={{0,1},{1,0},{2,3},{3,2},{4,5},{5,4},{6,7},{7,6},{8,9},{9,8},{10,11... | collective-permute-start | bytes 1769480 | tf_op jit(solution)/shard_map/ppermute | solution.py:138
  310.4 100.2 %collective-permute-start.7 = (bf16[100,512]{1,0:T(8,128)(2,1)S(1)}, bf16[100,512]{1,0:T(8,128)(2,1)S(1)}, u32[]{:S(2)}, u32[]{:S(2)}) collective-permute-start(bf16[100,512]{1,0:T(8,128)(2,1)S(1)} %constant_dynamic-slice_fusion.11), channel_id=1, source_target_pairs={{0,1},{1,0},{2,3},{3,2},{4,5},{5,4},{6,7},{7,6},{8,9},{9,8},{10,11... | collective-permute-start | bytes 307208 | tf_op jit(solution)/shard_map/ppermute | solution.py:138
  410.7 4.2 collective-permute-start.8
  415.0 4.2 collective-permute-start.9
  419.3 4.8 collective-permute-start.10
  424.1 9.0 %collective-permute-start.11 = (bf16[200,512]{1,0:T(8,128)(2,1)S(1)}, bf16[200,512]{1,0:T(8,128)(2,1)S(1)}, u32[]{:S(2)}, u32[]{:S(2)}) collective-permute-start(bf16[200,512]{1,0:T(8,128)(2,1)S(1)} %pad_maximum_fusion.20), channel_id=1, source_target_pairs={{0,4},{1,5},{2,6},{3,7},{4,0},{5,1},{6,2},{7,3},{8,12},{9,13},{10,... | collective-permute-start | bytes 614408 | tf_op jit(solution)/shard_map/ppermute | solution.py:138
  427.7 6.8 %collective-permute-start.26 = (bf16[288,512]{1,0:T(8,128)(2,1)S(1)}, bf16[288,512]{1,0:T(8,128)(2,1)S(1)}, u32[]{:S(2)}, u32[]{:S(2)}) collective-permute-start(bf16[288,512]{1,0:T(8,128)(2,1)S(1)} %constant_dynamic-slice_fusion.2), channel_id=1, source_target_pairs={{0,1},{1,0},{2,3},{3,2},{4,5},{5,4},{6,7},{7,6},{8,9},{9,8},{10,11... | collective-permute-start | bytes 884744 | tf_op jit(solution)/shard_map/ppermute | solution.py:138
  430.5 6.8 %collective-permute-start.16 = (bf16[288,512]{1,0:T(8,128)(2,1)S(1)}, bf16[288,512]{1,0:T(8,128)(2,1)S(1)}, u32[]{:S(2)}, u32[]{:S(2)}) collective-permute-start(bf16[288,512]{1,0:T(8,128)(2,1)S(1)} %constant_dynamic-slice_fusion.7), channel_id=1, source_target_pairs={{0,16},{8,24},{16,0},{24,8},{1,17},{9,25},{17,1},{25,9},{2,18},{10... | collective-permute-start | bytes 884744 | tf_op jit(solution)/shard_map/ppermute | solution.py:138
  433.3 23.3 %collective-permute-start.12 = (bf16[400,512]{1,0:T(8,128)(2,1)S(1)}, bf16[400,512]{1,0:T(8,128)(2,1)S(1)}, u32[]{:S(2)}, u32[]{:S(2)}) collective-permute-start(bf16[400,512]{1,0:T(8,128)(2,1)S(1)} %pad_maximum_fusion.13), channel_id=1, source_target_pairs={{0,2},{1,3},{2,0},{3,1},{4,6},{5,7},{6,4},{7,5},{8,10},{9,11},{10,... | collective-permute-start | bytes 1228808 | tf_op jit(solution)/shard_map/ppermute | solution.py:138
  434.7 12.3 %collective-permute-start.27 = (bf16[144,512]{1,0:T(8,128)(2,1)S(1)}, bf16[144,512]{1,0:T(8,128)(2,1)S(1)}, u32[]{:S(2)}, u32[]{:S(2)}) collective-permute-start(bf16[144,512]{1,0:T(8,128)(2,1)S(1)} %constant_dynamic-slice_fusion.1), channel_id=1, source_target_pairs={{0,2},{1,3},{2,0},{3,1},{4,6},{5,7},{6,4},{7,5},{8,10},{9,11},{10,... | collective-permute-start | bytes 442376 | tf_op jit(solution)/shard_map/ppermute | solution.py:138
  437.4 11.9 %collective-permute-start.17 = (bf16[144,512]{1,0:T(8,128)(2,1)S(1)}, bf16[144,512]{1,0:T(8,128)(2,1)S(1)}, u32[]{:S(2)}, u32[]{:S(2)}) collective-permute-start(bf16[144,512]{1,0:T(8,128)(2,1)S(1)} %constant_dynamic-slice_fusion.6), channel_id=1, source_target_pairs={{0,2},{1,3},{2,0},{3,1},{4,6},{5,7},{6,4},{7,5},{8,10},{9,11},{10,... | collective-permute-start | bytes 442376 | tf_op jit(solution)/shard_map/ppermute | solution.py:138
  447.1 6.4 %collective-permute-start.28 = (bf16[72,512]{1,0:T(8,128)(2,1)S(1)}, bf16[72,512]{1,0:T(8,128)(2,1)S(1)}, u32[]{:S(2)}, u32[]{:S(2)}) collective-permute-start(bf16[72,512]{1,0:T(8,128)(2,1)S(1)} %constant_dynamic-slice_fusion), channel_id=1, source_target_pairs={{0,4},{1,5},{2,6},{3,7},{4,0},{5,1},{6,2},{7,3},{8,12},{9,13},{10,... | collective-permute-start | bytes 221192 | tf_op jit(solution)/shard_map/ppermute | solution.py:138
  449.4 6.0 %collective-permute-start.18 = (bf16[72,512]{1,0:T(8,128)(2,1)S(1)}, bf16[72,512]{1,0:T(8,128)(2,1)S(1)}, u32[]{:S(2)}, u32[]{:S(2)}) collective-permute-start(bf16[72,512]{1,0:T(8,128)(2,1)S(1)} %constant_dynamic-slice_fusion.5), channel_id=1, source_target_pairs={{0,4},{1,5},{2,6},{3,7},{4,0},{5,1},{6,2},{7,3},{8,12},{9,13},{10,... | collective-permute-start | bytes 221192 | tf_op jit(solution)/shard_map/ppermute | solution.py:138
  453.5 5.4 %collective-permute-start.29 = (bf16[72,512]{1,0:T(8,128)(2,1)S(1)}, bf16[72,512]{1,0:T(8,128)(2,1)S(1)}, u32[]{:S(2)}, u32[]{:S(2)}) collective-permute-start(bf16[72,512]{1,0:T(8,128)(2,1)S(1)} %add_convert_fusion.20), channel_id=1, source_target_pairs={{0,4},{1,5},{2,6},{3,7},{4,0},{5,1},{6,2},{7,3},{8,12},{9,13},{10,... | collective-permute-start | bytes 221192 | tf_op jit(solution)/shard_map/ppermute | solution.py:138
  455.4 6.2 %collective-permute-start.19 = (bf16[72,512]{1,0:T(8,128)(2,1)S(1)}, bf16[72,512]{1,0:T(8,128)(2,1)S(1)}, u32[]{:S(2)}, u32[]{:S(2)}) collective-permute-start(bf16[72,512]{1,0:T(8,128)(2,1)S(1)} %add_convert_fusion.21), channel_id=1, source_target_pairs={{0,4},{1,5},{2,6},{3,7},{4,0},{5,1},{6,2},{7,3},{8,12},{9,13},{10,... | collective-permute-start | bytes 221192 | tf_op jit(solution)/shard_map/ppermute | solution.py:138
  456.8 22.0 %collective-permute-start.13 = (bf16[800,512]{1,0:T(8,128)(2,1)S(1)}, bf16[800,512]{1,0:T(8,128)(2,1)S(1)}, u32[]{:S(2)}, u32[]{:S(2)}) collective-permute-start(bf16[800,512]{1,0:T(8,128)(2,1)S(1)} %pad_maximum_fusion.7), channel_id=1, source_target_pairs={{0,8},{8,0},{16,24},{24,16},{1,9},{9,1},{17,25},{25,17},{2,10},{10... | collective-permute-start | bytes 2457608 | tf_op jit(solution)/shard_map/ppermute | solution.py:138
  458.9 6.6 %collective-permute-start.30 = (bf16[144,512]{1,0:T(8,128)(2,1)S(1)}, bf16[144,512]{1,0:T(8,128)(2,1)S(1)}, u32[]{:S(2)}, u32[]{:S(2)}) collective-permute-start(bf16[144,512]{1,0:T(8,128)(2,1)S(1)} %pad_maximum_fusion.24), channel_id=1, source_target_pairs={{0,2},{1,3},{2,0},{3,1},{4,6},{5,7},{6,4},{7,5},{8,10},{9,11},{10,... | collective-permute-start | bytes 442376 | tf_op jit(solution)/shard_map/ppermute | solution.py:138
  461.7 5.4 %collective-permute-start.20 = (bf16[144,512]{1,0:T(8,128)(2,1)S(1)}, bf16[144,512]{1,0:T(8,128)(2,1)S(1)}, u32[]{:S(2)}, u32[]{:S(2)}) collective-permute-start(bf16[144,512]{1,0:T(8,128)(2,1)S(1)} %pad_maximum_fusion.23), channel_id=1, source_target_pairs={{0,2},{1,3},{2,0},{3,1},{4,6},{5,7},{6,4},{7,5},{8,10},{9,11},{10,... | collective-permute-start | bytes 442376 | tf_op jit(solution)/shard_map/ppermute | solution.py:138
  465.6 6.8 %collective-permute-start.31 = (bf16[288,512]{1,0:T(8,128)(2,1)S(1)}, bf16[288,512]{1,0:T(8,128)(2,1)S(1)}, u32[]{:S(2)}, u32[]{:S(2)}) collective-permute-start(bf16[288,512]{1,0:T(8,128)(2,1)S(1)} %pad_maximum_fusion.15), channel_id=1, source_target_pairs={{0,1},{1,0},{2,3},{3,2},{4,5},{5,4},{6,7},{7,6},{8,9},{9,8},{10,11... | collective-permute-start | bytes 884744 | tf_op jit(solution)/shard_map/ppermute | solution.py:138
  467.2 10.0 %collective-permute-start.21 = (bf16[288,512]{1,0:T(8,128)(2,1)S(1)}, bf16[288,512]{1,0:T(8,128)(2,1)S(1)}, u32[]{:S(2)}, u32[]{:S(2)}) collective-permute-start(bf16[288,512]{1,0:T(8,128)(2,1)S(1)} %pad_maximum_fusion.14), channel_id=1, source_target_pairs={{0,16},{8,24},{16,0},{24,8},{1,17},{9,25},{17,1},{25,9},{2,18},{10... | collective-permute-start | bytes 884744 | tf_op jit(solution)/shard_map/ppermute | solution.py:138
  472.5 14.5 %collective-permute-start.32 = (bf16[576,512]{1,0:T(8,128)(2,1)S(1)}, bf16[576,512]{1,0:T(8,128)(2,1)S(1)}, u32[]{:S(2)}, u32[]{:S(2)}) collective-permute-start(bf16[576,512]{1,0:T(8,128)(2,1)S(1)} %pad_maximum_fusion.10), channel_id=1, source_target_pairs={{0,16},{8,24},{16,0},{24,8},{1,17},{9,25},{17,1},{25,9},{2,18},{10... | collective-permute-start | bytes 1769480 | tf_op jit(solution)/shard_map/ppermute | solution.py:138
  477.3 11.1 %collective-permute-start.22 = (bf16[576,512]{1,0:T(8,128)(2,1)S(1)}, bf16[576,512]{1,0:T(8,128)(2,1)S(1)}, u32[]{:S(2)}, u32[]{:S(2)}) collective-permute-start(bf16[576,512]{1,0:T(8,128)(2,1)S(1)} %pad_maximum_fusion.9), channel_id=1, source_target_pairs={{0,1},{1,0},{2,3},{3,2},{4,5},{5,4},{6,7},{7,6},{8,9},{9,8},{10,11... | collective-permute-start | bytes 1769480 | tf_op jit(solution)/shard_map/ppermute | solution.py:138
  488.4 6.9 %collective-permute-start.33 = (bf16[1152,512]{1,0:T(8,128)(2,1)}, bf16[1152,512]{1,0:T(8,128)(2,1)}, u32[]{:S(2)}, u32[]{:S(2)}) collective-permute-start(bf16[1152,512]{1,0:T(8,128)(2,1)} %pad_maximum_fusion.6), channel_id=1, source_target_pairs={{0,8},{8,0},{16,24},{24,16},{1,9},{9,1},{17,25},{25,17},{2,10},{10... | collective-permute-start | bytes 3538952 | tf_op jit(solution)/shard_map/ppermute | solution.py:138
  489.8 7.3 %collective-permute-start.23 = (bf16[1152,512]{1,0:T(8,128)(2,1)}, bf16[1152,512]{1,0:T(8,128)(2,1)}, u32[]{:S(2)}, u32[]{:S(2)}) collective-permute-start(bf16[1152,512]{1,0:T(8,128)(2,1)} %pad_maximum_fusion.5), channel_id=1, source_target_pairs={{0,8},{8,0},{16,24},{24,16},{1,9},{9,1},{17,25},{25,17},{2,10},{10... | collective-permute-start | bytes 3538952 | tf_op jit(solution)/shard_map/ppermute | solution.py:138
  (135 other events, 867.8 us)
Sparse Core Ops, SparseCore 0:
  243.3 164.1 all-reduce.3
